TPU v7x, 32 devices: a whole 2x2x4 slice. The times are simulated.
32 devices in a mesh: dp: 8 (over z, x), tp: 4 (over y, core).
Axes of the slice: x: 2, y: 2, z: 4, core: 2. Of those that a mesh axis runs over, the one named last changes fastest.
Arguments:
- tokens: bfloat16 [16384, 768], P(('dp', 'tp')), may hold values from -6 to 6
- first_gain: float32 [768], replicated, may hold values from 0.5 to 1.5
- first_bias: float32 [768], replicated, may hold values from -1 to 1
- qkv_weight: bfloat16 [768, 3, 768], P(None, None, 'tp'), may hold values from -0.21875 to 0.21875
- out_weight: bfloat16 [768, 768], P('tp'), may hold values from -0.875 to 0.875
- second_gain: float32 [768], replicated, may hold values from 0.5 to 1.5
- expert_norm_bias: float32 [768], replicated, may hold values from -1 to 1
- up_weight: bfloat16 [8, 768, 1536], P('dp'), may hold values from -0.21875 to 0.21875
- down_weight: bfloat16 [8, 1536, 768], P('dp'), may hold values from -0.21875 to 0.21875
- gate_value: float32 [16384], P(('dp', 'tp')), may hold values from 0.3 to 1
- expert_ids: int32 [16384], P(('dp', 'tp')), may hold values from 0 to 3, as said below
- slot_index: int32 [16384], P(('dp', 'tp')), may hold values from 0 to 255, as said below
- segment_ids: int32 [16384], P(('dp', 'tp')), may hold values from 0 to 1024, as said below
- cotangent: bfloat16 [16384, 768], P(('dp', 'tp')), may hold values from -15 to 15
Outputs:
- output: bfloat16 [16384, 768], P(('dp', 'tp'))
- grad_input: float32 [16384, 768], P(('dp', 'tp'))
- grad_first_gain: float32 [768], replicated
- grad_first_bias: float32 [768], replicated
- grad_qkv_weight: float32 [768, 3, 768], P(None, None, 'tp')
- grad_out_weight: float32 [768, 768], P('tp')
- grad_second_gain: float32 [768], replicated
- grad_second_bias: float32 [768], replicated
- grad_up_weight: float32 [8, 768, 1536], P('dp', None, 'tp')
- grad_down_weight: float32 [8, 1536, 768], P('dp', 'tp')
Inputs may be any that keep to these rules, and one draw needn't show every extreme that they name: `expert_ids`: in each aligned block of 512 tokens no expert is named more than 256 times, and some expert is named exactly 256 times. `slot_index`: in each aligned block of 512 tokens, the tokens that name one expert have distinct slots. `segment_ids`: within each packed row of 1024 tokens the ids start at 0 and never fall, distinct documents have distinct ids, and the last document of every packed row has the id 1024; in every packed row one document begins before position 256 and ends at or after position 768.
All inputs are finite; a program needn't handle non-finite values.
Results may differ from a plain program's by a relative error of at most 0.017.
Values may be sent and summed in bfloat16 or wider, within the bound.
No kernel may reach another device: no remote copies, remote signals or barrier semaphores. Data moves between devices by JAX's collectives and lax.ppermute only.
A program may use at most 128 MiB of HBM per device.

v0:
```python
import jax
import jax.numpy as jnp
from jax import lax
from jax.sharding import PartitionSpec as P

HEAD_DIM = 64
PACKED_LENGTH = 1024


EPSILON = 1e-05


def normalize(values, norm_gain, norm_bias):
    centre = jnp.mean(values, axis=-1, keepdims=True)
    shifted = values - centre
    inverse = lax.rsqrt(jnp.mean(shifted * shifted, axis=-1, keepdims=True) + EPSILON)
    scaled = shifted * inverse
    return (scaled * norm_gain + norm_bias, scaled, inverse)


def norm_backward(grad_normed, scaled, inverse, norm_gain):
    grad_scaled = grad_normed * norm_gain
    first_mean = jnp.mean(grad_scaled, axis=-1, keepdims=True)
    second_mean = jnp.mean(grad_scaled * scaled, axis=-1, keepdims=True)
    grad_values = inverse * (grad_scaled - first_mean - scaled * second_mean)
    return (grad_values, jnp.sum(grad_normed * scaled, axis=0), jnp.sum(grad_normed, axis=0))


def split_items(array, local_count):
    return array.reshape(-1, local_count, array.shape[1], array.shape[2])


def expert_forward(inputs, up_weight, down_weight):
    local_count = up_weight.shape[0]
    shaped = split_items(inputs, local_count)
    preact = jnp.einsum("secd,edf->secf", shaped, up_weight, preferred_element_type=jnp.float32)
    hidden = jax.nn.gelu(preact, approximate=False).astype(jnp.bfloat16)
    result = jnp.einsum(
        "secf,efd->secd", hidden, down_weight, preferred_element_type=jnp.float32
    ).astype(jnp.bfloat16)
    rows_here = inputs.shape[1]
    return (
        preact.reshape(inputs.shape[0], rows_here, -1),
        hidden.reshape(inputs.shape[0], rows_here, -1),
        result.reshape(inputs.shape[0], rows_here, -1),
    )


def expert_backward(preact, grad_result, up_weight, down_weight):
    local_count = up_weight.shape[0]
    grad_hidden = jnp.einsum(
        "secd,efd->secf",
        split_items(grad_result, local_count),
        down_weight,
        preferred_element_type=jnp.float32,
    )
    shaped_pre = split_items(preact, local_count)
    unused, pullback = jax.vjp(lambda value: jax.nn.gelu(value, approximate=False), shaped_pre)
    grad_preact = pullback(grad_hidden)[0].astype(jnp.bfloat16)
    grad_inputs = jnp.einsum(
        "secf,edf->secd", grad_preact, up_weight, preferred_element_type=jnp.float32
    ).astype(jnp.bfloat16)
    rows_here = preact.shape[1]
    return (
        grad_preact.reshape(preact.shape[0], rows_here, -1),
        grad_inputs.reshape(preact.shape[0], rows_here, -1),
    )


def expert_weight_grads(inputs, hidden, grad_result, grad_preact, local_count):
    grad_up = jnp.einsum(
        "secd,secf->edf",
        split_items(inputs, local_count),
        split_items(grad_preact, local_count),
        preferred_element_type=jnp.float32,
    )
    grad_down = jnp.einsum(
        "secf,secd->efd",
        split_items(hidden, local_count),
        split_items(grad_result, local_count),
        preferred_element_type=jnp.float32,
    )
    return (grad_up, grad_down)


def local(
    tokens,
    first_gain,
    first_bias,
    qkv_weight,
    out_weight,
    second_gain,
    expert_norm_bias,
    up_weight,
    down_weight,
    gate_value,
    expert_ids,
    slot_index,
    segment_ids,
    cotangent,
):
    tok_rows = tokens.shape[0]
    model_width = tokens.shape[1]
    local_width = qkv_weight.shape[2]
    heads_here = local_width // HEAD_DIM
    score_scale = HEAD_DIM ** (-0.5)
    residual = tokens.astype(jnp.float32)
    normed_one, scaled_one, inverse_one = normalize(residual, first_gain, first_bias)
    normed_one = normed_one.astype(jnp.bfloat16)
    rows_all, segments_all = (
        lax.all_gather(normed_one, "tp", axis=0, tiled=True),
        lax.all_gather(segment_ids, "tp", axis=0, tiled=True),
    )
    length_all = rows_all.shape[0]
    flat_qkv = qkv_weight.reshape(model_width, 3 * local_width)
    projected = jnp.dot(rows_all, flat_qkv, preferred_element_type=jnp.float32).astype(jnp.bfloat16)
    projected = projected.reshape(length_all, 3, heads_here, HEAD_DIM)
    queries = projected[:, 0]
    keys_all = projected[:, 1]
    values_all = projected[:, 2]
    block_rows = min(512, PACKED_LENGTH)
    block_count = length_all // block_rows
    row_offsets = jnp.arange(PACKED_LENGTH, dtype=jnp.int32)

    def block_scores(block_index):
        first_row = block_index * block_rows
        row_start = first_row // PACKED_LENGTH * PACKED_LENGTH
        query_blk = lax.dynamic_slice_in_dim(queries, first_row, block_rows, 0)
        keys_row = lax.dynamic_slice_in_dim(keys_all, row_start, PACKED_LENGTH, 0)
        scores = (
            jnp.einsum("qhd,khd->hqk", query_blk, keys_row, preferred_element_type=jnp.float32)
            * score_scale
        )
        query_segs = lax.dynamic_slice_in_dim(segments_all, first_row, block_rows, 0)
        key_segs = lax.dynamic_slice_in_dim(segments_all, row_start, PACKED_LENGTH, 0)
        query_pos = first_row + jnp.arange(block_rows, dtype=jnp.int32)
        key_pos = row_start + row_offsets
        allowed = (key_pos[None, :] <= query_pos[:, None]) & (
            key_segs[None, :] == query_segs[:, None]
        )
        return (query_blk, keys_row, row_start, jnp.where(allowed[None], scores, -1e30))

    def attend(block_index):
        unused, keys_row, row_start, masked = block_scores(block_index)
        highest = jnp.max(masked, axis=-1, keepdims=True)
        weight_params = jnp.exp(masked - highest)
        denominator = jnp.sum(weight_params, axis=-1, keepdims=True)
        probability = (weight_params / denominator).astype(jnp.bfloat16)
        values_row = lax.dynamic_slice_in_dim(values_all, row_start, PACKED_LENGTH, 0)
        result = jnp.einsum(
            "hqk,khd->qhd", probability, values_row, preferred_element_type=jnp.float32
        )
        return (result.astype(jnp.bfloat16), (highest + jnp.log(denominator))[..., 0])

    attended, log_total = lax.map(attend, jnp.arange(block_count, dtype=jnp.int32))
    attended = attended.reshape(length_all, local_width)
    branch = lax.psum_scatter(
        jnp.dot(attended, out_weight, preferred_element_type=jnp.float32).astype(jnp.bfloat16),
        "tp",
        scatter_dimension=0,
        tiled=True,
    ).astype(jnp.float32)
    middle = residual + branch
    normed_two, scaled_two, inverse_two = normalize(middle, second_gain, expert_norm_bias)
    normed_two = normed_two.astype(jnp.bfloat16)
    local_count = up_weight.shape[0]
    experts_all = lax.axis_size("dp") // 2
    capacity = 2 * tok_rows // experts_all
    places = expert_ids * capacity + slot_index
    cot_float = cotangent.astype(jnp.float32)
    grad_expert = (gate_value[:, None] * cot_float).astype(jnp.bfloat16)

    def dispatch(rows):
        buffer = jnp.zeros((experts_all * capacity, model_width), jnp.bfloat16).at[places].set(rows)
        paired = jnp.broadcast_to(
            buffer.reshape(experts_all, 1, capacity, model_width),
            (experts_all, 2, capacity, model_width),
        )
        return paired.reshape(2 * experts_all, capacity, model_width)

    def collect(buffer):
        shaped = buffer.reshape(experts_all, 2, capacity, model_width)
        first_part = shaped[:, 0].reshape(-1, model_width)[places].astype(jnp.float32)
        second_part = shaped[:, 1].reshape(-1, model_width)[places].astype(jnp.float32)
        return first_part + second_part

    inputs = lax.all_to_all(dispatch(normed_two), "dp", split_axis=0, concat_axis=0, tiled=True)
    preact, hidden, result = expert_forward(inputs, up_weight, down_weight)
    returned = lax.all_to_all(result, "dp", split_axis=0, concat_axis=0, tiled=True)
    recv_grads = lax.all_to_all(
        dispatch(grad_expert), "dp", split_axis=0, concat_axis=0, tiled=True
    )
    grad_preact, grad_inputs = expert_backward(preact, recv_grads, up_weight, down_weight)
    returned_grads = lax.all_to_all(grad_inputs, "dp", split_axis=0, concat_axis=0, tiled=True)
    output = (middle + gate_value[:, None] * collect(returned)).astype(jnp.bfloat16)
    grad_up_local, grad_down_local = expert_weight_grads(
        inputs, hidden, recv_grads, grad_preact, local_count
    )
    grad_up_weight, grad_down_weight = (
        lax.psum_scatter(
            grad_up_local.astype(jnp.bfloat16), "tp", scatter_dimension=2, tiled=True
        ).astype(jnp.float32),
        lax.psum_scatter(
            grad_down_local.astype(jnp.bfloat16), "tp", scatter_dimension=1, tiled=True
        ).astype(jnp.float32),
    )
    grad_mid_norm, grad_second_gain, grad_second_bias = norm_backward(
        collect(returned_grads), scaled_two, inverse_two, second_gain
    )
    grad_middle = cot_float + grad_mid_norm
    grad_branch = grad_middle.astype(jnp.bfloat16)
    grad_rows = lax.all_gather(grad_branch, "tp", axis=0, tiled=True)
    grad_out_weight = lax.dot_general(
        attended, grad_rows, (((0,), (0,)), ((), ())), preferred_element_type=jnp.float32
    )
    grad_attended = lax.dot_general(
        grad_rows, out_weight, (((1,), (1,)), ((), ())), preferred_element_type=jnp.float32
    )
    grad_attended = grad_attended.astype(jnp.bfloat16).reshape(length_all, heads_here, HEAD_DIM)

    def backward_block(carried, block_index):
        grad_keys, grad_values = carried
        first_row = block_index * block_rows
        query_blk, keys_row, row_start, masked = block_scores(block_index)
        values_row = lax.dynamic_slice_in_dim(values_all, row_start, PACKED_LENGTH, 0)
        probability = jnp.exp(masked - log_total[block_index][:, :, None])
        grad_out_blk = lax.dynamic_slice_in_dim(grad_attended, first_row, block_rows, 0)
        grad_probs = jnp.einsum(
            "qhd,khd->hqk", grad_out_blk, values_row, preferred_element_type=jnp.float32
        )
        inner_sum = jnp.sum(probability * grad_probs, axis=-1, keepdims=True)
        grad_scores = (probability * (grad_probs - inner_sum)).astype(jnp.bfloat16)
        grad_query = (
            jnp.einsum("hqk,khd->qhd", grad_scores, keys_row, preferred_element_type=jnp.float32)
            * score_scale
        )
        key_term = (
            jnp.einsum("hqk,qhd->khd", grad_scores, query_blk, preferred_element_type=jnp.float32)
            * score_scale
        )
        value_term = jnp.einsum(
            "hqk,qhd->khd",
            probability.astype(jnp.bfloat16),
            grad_out_blk,
            preferred_element_type=jnp.float32,
        )
        key_sum = lax.dynamic_slice_in_dim(grad_keys, row_start, PACKED_LENGTH, 0) + key_term
        value_sum = lax.dynamic_slice_in_dim(grad_values, row_start, PACKED_LENGTH, 0) + value_term
        grad_keys = lax.dynamic_update_slice_in_dim(grad_keys, key_sum, row_start, 0)
        grad_values = lax.dynamic_update_slice_in_dim(grad_values, value_sum, row_start, 0)
        return ((grad_keys, grad_values), grad_query)

    zeros_kv = jnp.zeros((length_all, heads_here, HEAD_DIM), jnp.float32)
    (grad_keys, grad_values), grad_queries = lax.scan(
        backward_block, (zeros_kv, zeros_kv), jnp.arange(block_count, dtype=jnp.int32)
    )
    grad_queries = grad_queries.reshape(length_all, heads_here, HEAD_DIM)
    grad_projected = jnp.stack([grad_queries, grad_keys, grad_values], axis=1).astype(jnp.bfloat16)
    grad_projected = grad_projected.reshape(length_all, 3 * local_width)
    grad_qkv_weight = lax.dot_general(
        rows_all, grad_projected, (((0,), (0,)), ((), ())), preferred_element_type=jnp.float32
    )
    grad_qkv_weight = grad_qkv_weight.reshape(model_width, 3, local_width)
    grad_normed_one = lax.psum_scatter(
        lax.dot_general(
            grad_projected, flat_qkv, (((1,), (1,)), ((), ())), preferred_element_type=jnp.float32
        ).astype(jnp.bfloat16),
        "tp",
        scatter_dimension=0,
        tiled=True,
    ).astype(jnp.float32)
    grad_in_norm, grad_first_gain, grad_first_bias = norm_backward(
        grad_normed_one, scaled_one, inverse_one, first_gain
    )
    grad_input = grad_middle + grad_in_norm
    grad_qkv_weight, grad_out_weight = lax.psum((grad_qkv_weight, grad_out_weight), "dp")
    grad_first_gain, grad_first_bias, grad_second_gain, grad_second_bias = lax.psum(
        (grad_first_gain, grad_first_bias, grad_second_gain, grad_second_bias), ("dp", "tp")
    )
    return (
        output,
        grad_input,
        grad_first_gain,
        grad_first_bias,
        grad_qkv_weight,
        grad_out_weight,
        grad_second_gain,
        grad_second_bias,
        grad_up_weight,
        grad_down_weight,
    )


def solution(mesh):
    placed = (
        P(("dp", "tp"), None),
        P(),
        P(),
        P(None, None, "tp"),
        P("tp", None),
        P(),
        P(),
        P("dp", None, None),
        P("dp", None, None),
        P(("dp", "tp")),
        P(("dp", "tp")),
        P(("dp", "tp")),
        P(("dp", "tp")),
        P(("dp", "tp"), None),
    )
    return jax.shard_map(
        local,
        mesh=mesh,
        in_specs=placed,
        out_specs=(
            P(("dp", "tp"), None),
            P(("dp", "tp"), None),
            P(),
            P(),
            P(None, None, "tp"),
            P("tp", None),
            P(),
            P(),
            P("dp", None, "tp"),
            P("dp", "tp", None),
        ),
        check_vma=False,
    )
```

profile of v0, /device:TPU:0, one launch (start us, length us, event | category | flops | bytes accessed | tf_op | source)
XLA Modules:
  0.0 838.4 jit_solution(14740759813080461215)
XLA Ops:
  13.3 6.3 all-gather
  19.6 25.0 %all-gather.4.cloned.1.call-done = bf16[2048,768]{1,0:T(8,128)(2,1)} async-done(((bf16[512,768]{1,0:T(8,128)(2,1)}), bf16[2048,768]{1,0:T(8,128)(2,1)}) %all-gather.4.cloned.1.call-update) | async-done | bytes 3145744 | tf_op jit(solution)/shard_map/all_gather | solution.py:111
  44.6 4.1 convolution_convert_fusion.2
  50.1 37.4 %while.32 = (s32[]{:T(128)}, bf16[4,512,3,64]{1,3,2,0:T(8,128)(2,1)}, f32[4,3,512]{2,1,0:T(4,128)}, s32[4]{0:T(128)S(1)}, bf16[2048,3,64]{0,2,1:T(8,128)(2,1)}, ...) while((s32[]{:T(128)}, ...), condition=%wide.region_5.6_spmd.clone, body=%wide.region_2.5_spmd.clone.sunk | while | flops 423198720 | bytes 25383376 | solution.py:155
  56.1 2.7 fusion.166
  61.3 2.4 fusion.164
  65.4 2.7 fusion.166
  70.6 2.4 fusion.164
  74.8 2.7 fusion.166
  80.0 2.4 fusion.164
  84.1 2.7 fusion.166
  91.2 2.7 convolution_convert_fusion.1
  94.0 38.1 %reduce-scatter.7.cloned.1.call-done = bf16[512,768]{1,0:T(8,128)(2,1)} async-done(((bf16[2048,768]{1,0:T(8,128)(2,1)}), bf16[512,768]{1,0:T(8,128)(2,1)}) %reduce-scatter.7.cloned.1.call-update) | async-done | bytes 786448 | tf_op jit(solution)/shard_map/reduce_scatter | solution.py:157
  135.0 4.8 scatter_custom_fusion
  139.9 3.4 broadcast_in_dim.117
  143.3 5.5 all-to-all-start
  148.8 3.9 scatter_custom_fusion.1
  152.7 66.9 %all-to-all-done = bf16[8,256,768]{2,1,0:T(8,128)(2,1)} async-done(((bf16[8,256,768]{2,1,0:T(8,128)(2,1)}), bf16[8,256,768]{2,1,0:T(8,128)(2,1)}, u32[]{:S(2)}, u32[]{:S(2)}) %all-to-all-start) | async-done | bytes 3145760 | tf_op jit(solution)/shard_map/all_to_all | solution.py:187
  219.6 3.3 broadcast_in_dim.119
  222.9 4.5 all-to-all-start.2
  227.4 9.9 %fusion.86 = f32[8,256,1536]{2,1,0:T(8,128)} fusion(bf16[8,256,768]{2,1,0:T(8,128)(2,1)} %all-to-all-done, bf16[1,768,1536]{2,1,0:T(8,128)(2,1)S(1)} %copy-done), kind=kOutput, calls=%fused_computation.118 | convolution fusion | flops 4831838208 | bytes 18087936 | tf_op jit(solution)/shard_map/secd,edf->secf/dot_general | solution.py:36
  237.3 60.2 %all-to-all-done.2 = bf16[8,256,768]{2,1,0:T(8,128)(2,1)} async-done(((bf16[8,256,768]{2,1,0:T(8,128)(2,1)}), bf16[8,256,768]{2,1,0:T(8,128)(2,1)}, u32[]{:S(2)}, u32[]{:S(2)}) %all-to-all-start.2) | async-done | bytes 3145760 | tf_op jit(solution)/shard_map/all_to_all | solution.py:190
  297.6 35.5 %fusion.57 = bf16[8,1,256,1536]{3,2,0,1:T(8,128)(2,1)S(1)} fusion(f32[8,256,1536]{2,1,0:T(8,128)} %fusion.86, bf16[8,256,768]{2,1,0:T(8,128)(2,1)} %all-to-all-done.2, bf16[1,1536,768]{2,1,0:T(8,128)(2,1)} %param.26), kind=kOutput, calls=%fused_computation.73 | convolution fusion | flops 5058330624 | bytes 24379392 | tf_op jit(solution)/shard_map/secd,efd->secf/dot_general | solution.py:51
  333.1 2.6 copy-done.43
  335.7 6.4 fusion.91
  342.1 4.1 all-to-all-start.3
  346.2 35.6 %fusion.88 = bf16[8,256,768]{2,1,0:T(8,128)(2,1)} fusion(bf16[1,1536,768]{2,1,0:T(8,128)(2,1)} %param.26, f32[8,256,1536]{2,1,0:T(8,128)} %fusion.86), kind=kOutput, calls=%fused_computation.120 | convolution fusion | flops 5037883392 | bytes 18087936 | tf_op jit(solution)/shard_map/secf,efd->secd/dot_general | solution.py:38
  381.8 35.2 %all-to-all-done.3 = bf16[8,256,768]{2,1,0:T(8,128)(2,1)S(1)} async-done(((bf16[8,256,768]{2,1,0:T(8,128)(2,1)}), bf16[8,256,768]{2,1,0:T(8,128)(2,1)S(1)}, u32[]{:S(2)}, u32[]{:S(2)}) %all-to-all-start.3) | async-done | bytes 3145760 | tf_op jit(solution)/shard_map/all_to_all | solution.py:194
  417.0 4.4 all-to-all-start.1
  423.7 2.7 gather_fusion.2
  426.4 2.7 gather_fusion.3
  429.1 62.6 %all-to-all-done.1 = bf16[8,256,768]{2,1,0:T(8,128)(2,1)} async-done(((bf16[8,256,768]{2,1,0:T(8,128)(2,1)}), bf16[8,256,768]{2,1,0:T(8,128)(2,1)}, u32[]{:S(2)}, u32[]{:S(2)}) %all-to-all-start.1) | async-done | bytes 3145760 | tf_op jit(solution)/shard_map/all_to_all | solution.py:189
  491.7 3.2 fusion.128
  494.9 4.8 gather_fusion
  499.8 2.7 gather_fusion.1
  502.5 2.9 multiply_reduce_fusion.1
  505.4 3.8 fusion.126
  509.5 8.3 fusion.78
  517.8 8.4 %copy.36 = bf16[1,768,1536]{1,0,2:T(2,128)(2,1)} copy(bf16[1,768,1536]{2,1,0:T(8,128)(2,1)S(1)} %fusion.78) | data formatting | bytes 4718592
  526.2 4.3 copy.55
  530.6 33.4 %fusion.81 = bf16[1,1536,768]{2,1,0:T(8,128)(2,1)} fusion(bf16[8,256,768]{2,1,0:T(8,128)(2,1)} %all-to-all-done.2, f32[8,256,1536]{2,1,0:T(8,128)} %fusion.86), kind=kOutput, calls=%fused_computation.105 | convolution fusion | flops 5037490176 | bytes 18087936 | tf_op jit(solution)/shard_map/secf,secd->efd/dot_general | solution.py:77
  564.3 4.2 convolution_convert_fusion.3
  570.0 96.3 %while.33 = (s32[]{:T(128)}, f32[2048,3,64]{0,2,1:T(8,128)S(1)}, f32[2048,3,64]{0,2,1:T(8,128)}, bf16[4,512,3,64]{1,0,3,2:T(4,128)(2,1)}, s32[4]{0:T(128)S(1)}, ...) while((s32[]{:T(128)}, f32[2048,3,64]{0,2,1:T(8,128)S(1)}, ...), condition=%wide.region_15.16_spmd.clone, body=%wide.region_13.15_spmd.clone.sunk | while | flops 1032585216 | bytes 61747784 | solution.py:254
  575.6 4.0 fusion.177
  579.6 2.5 multiply_reduce_fusion.5
  586.1 8.0 dynamic_update_slice.51
  599.7 4.0 fusion.177
  603.7 2.5 multiply_reduce_fusion.5
  610.2 8.0 dynamic_update_slice.51
  623.8 4.0 fusion.177
  627.8 2.5 multiply_reduce_fusion.5
  634.2 8.0 dynamic_update_slice.51
  647.8 4.0 fusion.177
  651.8 2.5 multiply_reduce_fusion.5
  658.3 8.0 dynamic_update_slice.51
  671.9 4.0 convolution_convert_fusion
  676.2 3.7 fusion.129
  679.9 5.2 fusion.76
  686.9 3.0 copy.37
  694.3 17.7 %reduce-scatter.9.cloned.1.call-done = bf16[512,768]{1,0:T(8,128)(2,1)} async-done(((bf16[2048,768]{1,0:T(8,128)(2,1)}), bf16[512,768]{1,0:T(8,128)(2,1)}) %reduce-scatter.9.cloned.1.call-update) | async-done | bytes 786448 | tf_op jit(solution)/shard_map/reduce_scatter | solution.py:264
  714.1 43.2 %all-reduce = (f32[768]{0:T(1024)}, f32[768]{0:T(1024)}, f32[768]{0:T(1024)}, f32[768]{0:T(1024)}) all-reduce(f32[768]{0:T(1024)S(1)} %get-tuple-element.327, f32[768]{0:T(1024)S(1)} %get-tuple-element.331, f32[768]{0:T(1024)S(1)} %copy-done.33, f32[768]{0:T(1024)S(1)} %copy-done.34), channel_id=1, replica_groups=mesh['dp'=8,'tp'=4] {'dp','tp'}, use_global_device_ids=true, to_apply=%region_20.21 | all-reduce | flops 3072 | bytes 24576 | tf_op jit(solution)/shard_map/psum | solution.py:277
  757.2 3.3 fusion.107
  760.6 65.9 %all-reduce.4.cloned.1.call-done = (f32[768,3,192]{0,2,1:T(8,128)}, f32[192,768]{1,0:T(8,128)}) async-done(((f32[768,3,192]{0,2,1:T(8,128)}, f32[192,768]{1,0:T(8,128)}), (f32[768,3,192]{0,2,1:T(8,128)}, f32[192,768]{1,0:T(8,128)})) %all-reduce.4.cloned.1.call-update) | async-done | bytes 2359312 | tf_op jit(solution)/shard_map/psum | solution.py:276
  826.4 2.8 copy.86
  (235 shorter events, 78.5 us)
Async XLA Ops:
  7.2 220.2 %copy-start = (bf16[1,768,1536]{2,1,0:T(8,128)(2,1)S(1)}, bf16[1,768,1536]{2,1,0:T(8,128)(2,1)}, u32[]{:S(2)}) copy-start(bf16[1,768,1536]{2,1,0:T(8,128)(2,1)} %param.25) | copy-start | bytes 7077892
  7.2 37.4 %all-gather.4.cloned.1.call-start = ((), (), s32[]{:S(2)}) async-start(), calls=%async_computation.8 | async-start | bytes 3932160 | tf_op jit(solution)/shard_map/all_gather | solution.py:111
  8.7 1.5 copy-start.22
  10.2 0.6 copy-start.29
  13.2 118.8 %reduce-scatter.7.cloned.1.call-start = ((), (), s32[]{:S(2)}) async-start(), calls=%async_computation.9 | async-start | bytes 3932160 | tf_op jit(solution)/shard_map/reduce_scatter | solution.py:157
  50.1 41.1 %copy-start.20 = (bf16[192,768]{1,0:T(8,128)(2,1)S(1)}, bf16[192,768]{1,0:T(8,128)(2,1)}, u32[]{:S(2)}) copy-start(bf16[192,768]{1,0:T(8,128)(2,1)} %param.22) | copy-start | bytes 884740
  51.9 4.1 copy-start.12
  61.3 4.1 copy-start.12
  70.6 4.1 copy-start.12
  80.0 4.1 copy-start.12
  87.5 0.9 copy-start.5
  87.5 6.4 copy-start.18
  90.1 3.8 copy-start.40
  90.1 3.8 copy-start.41
  90.1 41.9 %copy-start.2 = (bf16[512,768]{1,0:T(8,128)(2,1)S(1)}, bf16[512,768]{1,0:T(8,128)(2,1)}, u32[]{:S(2)}) copy-start(bf16[512,768]{1,0:T(8,128)(2,1)} %param.18) | copy-start | bytes 2359300
  90.3 0.9 copy-start.10
  91.2 43.8 %copy-start.26 = (f32[768]{0:T(1024)S(1)}, f32[768]{0:T(1024)}, u32[]{:S(2)}) copy-start(f32[768]{0:T(1024)} %param.23) | copy-start | bytes 9220
  91.2 43.8 %copy-start.39 = (f32[768]{0:T(1024)S(1)}, f32[768]{0:T(1024)}, u32[]{:S(2)}) copy-start(f32[768]{0:T(1024)} %param.24) | copy-start | bytes 9220
  94.0 54.8 %copy-start.35 = (s32[512]{0:T(512)}, s32[512]{0:T(512)S(1)}, u32[]{:S(2)}) copy-start(s32[512]{0:T(512)S(1)} %compare_select_fusion) | copy-start | bytes 6148
  133.5 9.8 %copy-start.24 = (f32[512]{0:T(512)}, f32[512]{0:T(512)S(1)}, u32[]{:S(2)}) copy-start(f32[512]{0:T(512)S(1)} %broadcast_multiply_fusion.4) | copy-start | bytes 6148
  135.0 8.2 copy-start.31
  139.9 8.9 %copy-start.14 = (bf16[512,768]{1,0:T(8,128)(2,1)S(1)}, bf16[512,768]{1,0:T(8,128)(2,1)}, u32[]{:S(2)}) copy-start(bf16[512,768]{1,0:T(8,128)(2,1)} %param.31) | copy-start | bytes 2359300
  139.9 8.9 %copy-start.37 = (f32[512]{0:T(512)S(1)}, f32[512]{0:T(512)}, u32[]{:S(2)}) copy-start(f32[512]{0:T(512)} %param.27) | copy-start | bytes 6148
  143.3 76.3 %all-to-all-start = ((bf16[8,256,768]{2,1,0:T(8,128)(2,1)}), bf16[8,256,768]{2,1,0:T(8,128)(2,1)}, u32[]{:S(2)}, u32[]{:S(2)}) async-start(bf16[8,256,768]{2,1,0:T(8,128)(2,1)} %bitcast.250), calls=%async_computation.1 | async-start | bytes 6291456 | tf_op jit(solution)/shard_map/all_to_all | solution.py:187
  222.9 74.6 %all-to-all-start.2 = ((bf16[8,256,768]{2,1,0:T(8,128)(2,1)}), bf16[8,256,768]{2,1,0:T(8,128)(2,1)}, u32[]{:S(2)}, u32[]{:S(2)}) async-start(bf16[8,256,768]{2,1,0:T(8,128)(2,1)} %bitcast.251), calls=%async_computation.3 | async-start | bytes 6291456 | tf_op jit(solution)/shard_map/all_to_all | solution.py:190
  333.1 2.6 copy-start.43
  342.1 74.9 %all-to-all-start.3 = ((bf16[8,256,768]{2,1,0:T(8,128)(2,1)}), bf16[8,256,768]{2,1,0:T(8,128)(2,1)S(1)}, u32[]{:S(2)}, u32[]{:S(2)}) async-start(bf16[8,256,768]{2,1,0:T(8,128)(2,1)} %fusion.91), calls=%async_computation.4 | async-start | bytes 6291456 | tf_op jit(solution)/shard_map/all_to_all | solution.py:194
  381.8 39.8 %copy-start.36 = (s32[512]{0:T(512)S(1)}, s32[512]{0:T(512)}, u32[]{:S(2)}) copy-start(s32[512]{0:T(512)} %copy-done.35) | copy-start | bytes 6148
  417.0 4.5 copy-start.9
  417.0 74.7 %all-to-all-start.1 = ((bf16[8,256,768]{2,1,0:T(8,128)(2,1)}), bf16[8,256,768]{2,1,0:T(8,128)(2,1)}, u32[]{:S(2)}, u32[]{:S(2)}) async-start(bf16[8,256,768]{2,1,0:T(8,128)(2,1)} %fusion.88), calls=%async_computation.2 | async-start | bytes 6291456 | tf_op jit(solution)/shard_map/all_to_all | solution.py:189
  421.5 142.8 %all-gather.6.cloned.1.call-start = ((), (), s32[]{:S(2)}) async-start(), calls=%async_computation.10 | async-start | bytes 3932160 | tf_op jit(solution)/shard_map/all_gather | solution.py:212
  494.9 7.5 copy-start.3
  494.9 7.5 copy-start.7
  494.9 7.5 copy-start.25
  494.9 7.5 copy-start.27
  494.9 7.5 copy-start.32
  499.8 5.7 copy-start.38
  509.3 175.9 %reduce-scatter.13.cloned.1.call-start = ((), (), s32[]{:S(2)}) async-start(), calls=%async_computation.13 | async-start | bytes 2949120
  530.5 33.8 %copy-start.21 = (bf16[192,768]{1,0:T(8,128)(2,1)S(1)}, bf16[192,768]{1,0:T(8,128)(2,1)}, u32[]{:S(2)}) copy-start(bf16[192,768]{1,0:T(8,128)(2,1)} %param.22) | copy-start | bytes 884740
  530.5 161.6 %reduce-scatter.11.cloned.1.call-start = ((), (), s32[]{:S(2)}) async-start(), calls=%async_computation.12 | async-start | bytes 2949120 | tf_op jit(solution)/shard_map/reduce_scatter | solution.py:203
  564.0 6.0 copy-start.6
  564.0 6.0 copy-start.8
  564.0 6.0 copy-start.19
  564.0 148.1 %reduce-scatter.9.cloned.1.call-start = ((), (), s32[]{:S(2)}) async-start(), calls=%async_computation.11 | async-start | bytes 3932160 | tf_op jit(solution)/shard_map/reduce_scatter | solution.py:264
  573.2 2.4 copy-start.17
  575.6 4.0 copy-start.13
  597.3 2.4 copy-start.17
  599.7 4.0 copy-start.13
  621.4 2.4 copy-start.17
  623.8 4.0 copy-start.13
  645.4 2.4 copy-start.17
  647.8 4.0 copy-start.13
  668.4 3.5 copy-start.42
  670.4 1.5 copy-start.15
  671.9 4.4 copy-start.11
  675.9 4.0 copy-start.16
  675.9 150.5 %all-reduce.4.cloned.1.call-start = ((), (), s32[]{:S(2)}) async-start(), calls=%async_computation.14 | async-start | bytes 4718592 | tf_op jit(solution)/shard_map/psum | solution.py:276
  685.1 27.0 %copy-start.4 = (bf16[512,768]{1,0:T(8,128)(2,1)S(1)}, bf16[512,768]{1,0:T(8,128)(2,1)}, u32[]{:S(2)}) copy-start(bf16[512,768]{1,0:T(8,128)(2,1)} %param.18) | copy-start | bytes 2359300
  685.1 27.0 %copy-start.23 = (f32[512]{0:T(512)S(1)}, f32[512]{0:T(512)}, u32[]{:S(2)}) copy-start(f32[512]{0:T(512)} %copy-done.22) | copy-start | bytes 6148
  685.1 27.0 %copy-start.28 = (f32[768]{0:T(1024)S(1)}, f32[768]{0:T(1024)}, u32[]{:S(2)}) copy-start(f32[768]{0:T(1024)} %param.19) | copy-start | bytes 9220
  685.1 27.0 %copy-start.30 = (f32[512]{0:T(512)S(1)}, f32[512]{0:T(512)}, u32[]{:S(2)}) copy-start(f32[512]{0:T(512)} %copy-done.29) | copy-start | bytes 6148
  685.1 29.0 %copy-start.33 = (f32[768]{0:T(1024)S(1)}, f32[768]{0:T(1024)}, u32[]{:S(2)}) copy-start(f32[768]{0:T(1024)} %get-tuple-element.324) | copy-start | bytes 9220
  685.1 29.0 %copy-start.34 = (f32[768]{0:T(1024)S(1)}, f32[768]{0:T(1024)}, u32[]{:S(2)}) copy-start(f32[768]{0:T(1024)} %get-tuple-element.329) | copy-start | bytes 9220
  689.9 141.3 %copy-start.1 = (bf16[1,768,1536]{2,1,0:T(8,128)(2,1)S(1)}, bf16[1,768,1536]{2,1,0:T(8,128)(2,1)}, u32[]{:S(2)}) copy-start(bf16[1,768,1536]{2,1,0:T(8,128)(2,1)} %param.25) | copy-start | bytes 7077892
Sparse Core Ops, SparseCore 0:
  13.3 31.2 all-gather.3
  94.0 37.9 reduce-scatter.6
  509.4 26.6 all-gather.5
  538.6 33.0 reduce-scatter.12
  574.1 33.0 reduce-scatter.10
  676.0 36.0 reduce-scatter.8
  716.3 110.1 all-reduce.3
where the time goes:
time: 850 us; the launch traced here: 838 us
  waiting for transfers between devices  372 us (44%)
  matrix products  211 us (25%)
  local copies, waits for them, and re-layouts  102 us (12%)
  other arithmetic  56.2 us (7%)
  blocking collectives  49.5 us (6%)
  starting transfers between devices  19.4 us (2%)
  between operations  15.1 us (2%)
  loops' own time  13.6 us (2%)
    all_to_all x1, waiting for transfers between devices, local(): lax.all_to_all(dispatch(normed_two), 'dp', split_axis=0, concat_axis=0, t...  66.9 us
    psum x1, waiting for transfers between devices, local(): lax.psum((grad_qkv_weight, grad_out_weight), 'dp')  65.9 us
    all_to_all x1, waiting for transfers between devices, local(): lax.all_to_all(result, 'dp', split_axis=0, concat_axis=0, tiled=True)  62.6 us
    all_to_all x1, waiting for transfers between devices, local(): lax.all_to_all(dispatch(grad_expert), 'dp', split_axis=0, concat_axis=0,...  60.2 us
    psum x1, blocking collectives, local(): lax.psum((grad_first_gain, grad_first_bias, grad_second_gain, grad_second...  43.2 us
    reduce_scatter x1, waiting for transfers between devices, local(): lax.psum_scatter(jnp.dot(attended, out_weight, preferred_element_type=jnp...  38.1 us
    dot_general x1, matrix products, expert_forward(): jnp.einsum('secf,efd->secd', hidden, down_weight, preferred_element_type=...  35.6 us
    dot_general x1, matrix products, expert_backward(): jnp.einsum('secd,efd->secf', split_items(grad_result, local_count), down_...  35.5 us
  transfers between devices with their start and end apart: 11, of which 8 were waited for; matrix products, arithmetic and copies ran while one was open for 28% of the time, Pallas kernels for 0%

commit v1 on v0

v1 whole, which is shorter than its diff:
```python
import functools

import jax
import jax.numpy as jnp
from jax import lax
from jax.experimental import pallas as pl
from jax.experimental.pallas import tpu as pltpu
from jax.sharding import PartitionSpec as P

HEAD_DIM = 64
PACKED_LENGTH = 1024
EPSILON = 1e-05
BF = jnp.bfloat16
F32 = jnp.float32
MASKED = -1e30
CHUNKS = 4


def dot(a, b, ca, cb):
    return lax.dot_general(a, b, (((ca,), (cb,)), ((), ())), preferred_element_type=F32)


def params(mib, **kw):
    return pltpu.CompilerParams(vmem_limit_bytes=mib * 1024 * 1024, **kw)


def cost(flops, nbytes):
    return pl.CostEstimate(flops=int(flops), bytes_accessed=int(nbytes), transcendentals=0)


def vmem():
    return pl.BlockSpec(memory_space=pltpu.VMEM)


def smem():
    return pl.BlockSpec(memory_space=pltpu.SMEM)


def norm_parts(values):
    centre = jnp.mean(values, axis=-1, keepdims=True)
    shifted = values - centre
    inverse = lax.rsqrt(jnp.mean(shifted * shifted, axis=-1, keepdims=True) + EPSILON)
    return shifted * inverse, inverse


def norm_back(grad_normed, scaled, inverse, gain):
    grad_scaled = grad_normed * gain
    first = jnp.mean(grad_scaled, axis=-1, keepdims=True)
    second = jnp.mean(grad_scaled * scaled, axis=-1, keepdims=True)
    return inverse * (grad_scaled - first - scaled * second)


def onehot(places, slots):
    rows = lax.broadcasted_iota(jnp.int32, (slots, places.shape[1]), 0)
    return jnp.where(rows == places, 1.0, 0.0).astype(BF)


def put_chunks(rows, places, outs):
    size = outs[0].shape[0]
    table = onehot(places, size * len(outs))
    for index, out in enumerate(outs):
        out[...] = dot(table[index * size : (index + 1) * size], rows, 1, 0).astype(BF)


def take_chunks(chunks, places):
    size = chunks[0].shape[0]
    table = onehot(places, size * len(chunks))
    total = None
    for index, chunk in enumerate(chunks):
        part = dot(table[index * size : (index + 1) * size], chunk[...], 0, 0)
        total = part if total is None else total + part
    return total


def grad_dispatch_kernel(cot_ref, gate_ref, places_ref, *outs):
    rows = (gate_ref[...] * cot_ref[...].astype(F32)).astype(BF)
    put_chunks(rows, places_ref[...], outs)


def grad_dispatch(cotangent, gate, places):
    tokens, width = cotangent.shape
    size = 2 * tokens // CHUNKS
    return pl.pallas_call(
        grad_dispatch_kernel,
        out_shape=[jax.ShapeDtypeStruct((size, width), BF)] * CHUNKS,
        compiler_params=params(32),
        cost_estimate=cost(4 * tokens * tokens * width, 6 * tokens * width),
        name="grad_dispatch",
    )(cotangent, gate, places)


def attend_kernel(
    first, heads, info, own, oth, gain, bias, weight, segr, segc, *refs
):
    if first:
        rows_out, att, probs, qkv, recip, mask, rows = refs
    else:
        att, probs, qkv, recip, mask = refs
        rows = own
    length = PACKED_LENGTH
    step = pl.program_id(0)
    width = heads * HEAD_DIM
    blk = att.shape[1] // 4
    half = length // 2

    @pl.when(step == 0)
    def start():
        if first:
            parity = info[0]
            for ref, place in ((own, parity), (oth, 1 - parity)):
                scaled, unused = norm_parts(ref[...].astype(F32))
                normed = (scaled * gain[...] + bias[...]).astype(BF)
                rows[pl.ds(pl.multiple_of(place * half, half), half), :] = normed
            rows_out[...] = rows[...]
        projected = dot(weight[...], rows[...], 1, 1).astype(BF)
        qkv[...] = projected
        qkv[0:width, :] = projected[0:width] * jnp.asarray(HEAD_DIM**-0.5, BF)

    for index in range(4):

        @pl.when(step == index)
        def block(index=index):
            upto = (index + 1) * blk
            cols = slice(index * blk, upto)
            keypos = lax.broadcasted_iota(jnp.int32, (upto, blk), 0)
            querypos = lax.broadcasted_iota(jnp.int32, (upto, blk), 1) + index * blk
            allowed = (segc[0:upto, :] == segr[:, cols]) & (keypos <= querypos)
            mask[0:upto, :] = jnp.where(allowed, 0.0, MASKED)
            for head in range(heads):
                at = head * HEAD_DIM
                query = qkv[at : at + HEAD_DIM, cols]
                keys = qkv[width + at : width + at + HEAD_DIM, 0:upto]
                values = qkv[2 * width + at : 2 * width + at + HEAD_DIM, 0:upto]
                scores = dot(keys, query, 0, 0) + mask[0:upto, :]
                highest = jnp.max(scores, axis=0, keepdims=True)
                weights = jnp.exp(scores - highest)
                inverse = 1.0 / jnp.sum(weights, axis=0, keepdims=True)
                low = weights.astype(BF)
                probs[head, 0:upto, :] = low
                result = dot(values, low, 1, 0) * inverse
                att[at : at + HEAD_DIM, cols] = result.astype(BF)
                recip[head : head + 1, cols] = inverse


def attend(first, info, own, oth, gain, bias, weight, segr, segc):
    length = PACKED_LENGTH
    model = own.shape[1]
    width = weight.shape[0] // 3
    heads = width // HEAD_DIM
    blk = length // 4
    outs = [
        jax.ShapeDtypeStruct((width, length), BF),
        jax.ShapeDtypeStruct((heads, length, length), BF),
        jax.ShapeDtypeStruct((3 * width, length), BF),
        jax.ShapeDtypeStruct((8, length), F32),
    ]
    whole = lambda shape: pl.BlockSpec(shape, lambda i: (0,) * len(shape))
    out_specs = [
        whole((width, length)),
        pl.BlockSpec((heads, length, blk), lambda i: (0, 0, i)),
        whole((3 * width, length)),
        whole((8, length)),
    ]
    scratch = [pltpu.VMEM((length, blk), F32)]
    if first:
        outs = [jax.ShapeDtypeStruct((length, model), BF)] + outs
        out_specs = [whole((length, model))] + out_specs
        scratch = scratch + [pltpu.VMEM((length, model), BF)]
    operands = (own, oth, gain, bias, weight, segr, segc)
    return pl.pallas_call(
        functools.partial(attend_kernel, first, heads),
        out_shape=outs,
        grid=(4,),
        in_specs=[smem()] + [whole(o.shape) for o in operands],
        out_specs=out_specs,
        scratch_shapes=scratch,
        compiler_params=params(40, dimension_semantics=("arbitrary",)),
        cost_estimate=cost(
            6 * length * model * width + 8 * heads * length * length * HEAD_DIM,
            2 * heads * length * length + 6 * length * model,
        ),
        name="attend",
    )(info, *operands)


def project_kernel(info, att_a, att_b, out_a, out_b, kept, sent):
    half = kept.shape[0]
    parity = info[0]
    for ref, place in ((sent, 1 - parity), (kept, parity)):
        cols = pl.ds(pl.multiple_of(place * half, half), half)
        total = dot(att_a[:, cols], out_a[...], 0, 0) + dot(att_b[:, cols], out_b[...], 0, 0)
        ref[...] = total.astype(ref.dtype)


def project(info, att_a, att_b, out_a, out_b):
    width, length = att_a.shape
    model = out_a.shape[1]
    return pl.pallas_call(
        project_kernel,
        out_shape=[
            jax.ShapeDtypeStruct((length // 2, model), F32),
            jax.ShapeDtypeStruct((length // 2, model), BF),
        ],
        in_specs=[smem()] + [vmem()] * 4,
        out_specs=[vmem()] * 2,
        compiler_params=params(32),
        cost_estimate=cost(4 * length * model * width, 6 * length * model),
        name="project",
    )(info, att_a, att_b, out_a, out_b)


def middle_kernel(tokens, kept, received, gain, bias, places, middle, *outs):
    values = tokens[...].astype(F32) + (kept[...] + received[...].astype(F32))
    middle[...] = values
    scaled, unused = norm_parts(values)
    normed = (scaled * gain[...] + bias[...]).astype(BF)
    put_chunks(normed, places[...], outs)


def middle_call(tokens, kept, received, gain, bias, places):
    count, width = tokens.shape
    size = 2 * count // CHUNKS
    return pl.pallas_call(
        middle_kernel,
        out_shape=[jax.ShapeDtypeStruct((count, width), F32)]
        + [jax.ShapeDtypeStruct((size, width), BF)] * CHUNKS,
        compiler_params=params(32),
        cost_estimate=cost(4 * count * count * width, 14 * count * width),
        name="middle",
    )(tokens, kept, received, gain, bias, places)


def gelu_parts(x):
    z = jnp.abs(x) * (0.5**0.5)
    t = 1.0 / (1.0 + 0.3275911 * z)
    poly = t * (
        0.254829592
        + t * (-0.284496736 + t * (1.421413741 + t * (-1.453152027 + t * 1.061405429)))
    )
    bell = jnp.exp(-0.5 * x * x)
    tail = 0.5 * poly * bell
    phi = jnp.where(x >= 0.0, 1.0 - tail, tail)
    return x * phi, phi + x * bell * 0.3989422804014327


def expert_kernel(tiles, inputs, grads, *refs):
    ups, downs = refs[:tiles], refs[tiles : 2 * tiles]
    hidden, gpre, result, total = refs[2 * tiles :]
    step = pl.program_id(0)
    for tile in range(tiles):

        @pl.when(step == tile)
        def work(tile=tile):
            up, down = ups[tile][...], downs[tile][...]
            preact = dot(inputs[...], up, 1, 0)
            ghidden = dot(grads[...], down, 1, 1)
            act, slope = gelu_parts(preact)
            hidden[...] = act.astype(BF)
            low = (ghidden * slope).astype(BF)
            gpre[...] = low
            part = dot(low, up, 1, 1)
            if tile == 0:
                total[...] = part
            elif tile < tiles - 1:
                total[...] += part
            else:
                result[...] = (total[...] + part).astype(BF)


def expert(inputs, grads, ups, downs):
    rows, model = inputs.shape
    tiles = len(ups)
    tile = ups[0].shape[1]
    whole = lambda shape: pl.BlockSpec(shape, lambda i: (0,) * len(shape))
    return pl.pallas_call(
        functools.partial(expert_kernel, tiles),
        out_shape=[
            jax.ShapeDtypeStruct((rows, tiles * tile), BF),
            jax.ShapeDtypeStruct((rows, tiles * tile), BF),
            jax.ShapeDtypeStruct((rows, model), BF),
        ],
        grid=(tiles,),
        in_specs=[whole((rows, model))] * 2 + [whole(w.shape) for w in (*ups, *downs)],
        out_specs=[
            pl.BlockSpec((rows, tile), lambda i: (0, i)),
            pl.BlockSpec((rows, tile), lambda i: (0, i)),
            whole((rows, model)),
        ],
        scratch_shapes=[pltpu.VMEM((rows, model), F32)],
        compiler_params=params(48, dimension_semantics=("arbitrary",)),
        cost_estimate=cost(
            6 * rows * model * tile * tiles, 4 * model * tile * tiles + 4 * rows * tile * tiles
        ),
        name="expert",
    )(inputs, grads, *ups, *downs)


def expert_weights_kernel(tiles, *refs):
    n = CHUNKS
    inputs, grads, hiddens, gpres = refs[:n], refs[n : 2 * n], refs[2 * n : 3 * n], refs[3 * n : 4 * n]
    down = refs[4 * n]
    results = refs[4 * n + 1 : 5 * n + 1]
    gup, gdown = refs[5 * n + 1 : 5 * n + 3]
    totals = refs[5 * n + 3 :]
    step = pl.program_id(0)
    up_sum = None
    down_sum = None
    for index in range(n):
        hid = hiddens[index][...]
        up_part = dot(inputs[index][...], gpres[index][...], 0, 0)
        down_part = dot(hid, grads[index][...], 0, 0)
        up_sum = up_part if up_sum is None else up_sum + up_part
        down_sum = down_part if down_sum is None else down_sum + down_part
        part = dot(hid, down[0], 1, 0)

        @pl.when(step == 0)
        def first(index=index, part=part):
            totals[index][...] = part

        @pl.when((step > 0) & (step < tiles - 1))
        def between(index=index, part=part):
            totals[index][...] += part

        @pl.when(step == tiles - 1)
        def last(index=index, part=part):
            results[index][...] = (totals[index][...] + part).astype(BF)

    gup[0] = up_sum.astype(BF)
    gdown[0] = down_sum.astype(BF)


def expert_weights(inputs, grads, hiddens, gpres, downs):
    rows, model = inputs[0].shape
    tiles = len(downs)
    tile = downs[0].shape[0]
    down = jnp.stack(downs)
    whole = lambda shape: pl.BlockSpec(shape, lambda i: (0,) * len(shape))
    return pl.pallas_call(
        functools.partial(expert_weights_kernel, tiles),
        out_shape=[jax.ShapeDtypeStruct((rows, model), BF)] * CHUNKS
        + [
            jax.ShapeDtypeStruct((tiles, model, tile), BF),
            jax.ShapeDtypeStruct((tiles, tile, model), BF),
        ],
        grid=(tiles,),
        in_specs=[whole((rows, model))] * (2 * CHUNKS)
        + [pl.BlockSpec((rows, tile), lambda i: (0, i))] * (2 * CHUNKS)
        + [pl.BlockSpec((1, tile, model), lambda i: (i, 0, 0))],
        out_specs=[whole((rows, model))] * CHUNKS
        + [
            pl.BlockSpec((1, model, tile), lambda i: (i, 0, 0)),
            pl.BlockSpec((1, tile, model), lambda i: (i, 0, 0)),
        ],
        scratch_shapes=[pltpu.VMEM((rows, model), F32)] * CHUNKS,
        compiler_params=params(48, dimension_semantics=("arbitrary",)),
        cost_estimate=cost(
            6 * CHUNKS * rows * model * tile * tiles, 8 * model * tile * tiles
        ),
        name="expert_weights",
    )(*inputs, *grads, *hiddens, *gpres, down)


def second_back_kernel(*refs):
    chunks = refs[:CHUNKS]
    middle, cot, gain, places, gmid, gbranch, gvec = refs[CHUNKS:]
    grad = take_chunks(chunks, places[...])
    scaled, inverse = norm_parts(middle[...])
    total = cot[...].astype(F32) + norm_back(grad, scaled, inverse, gain[...])
    gmid[...] = total
    gbranch[...] = total.astype(BF)
    gvec[...] = jnp.zeros_like(gvec)
    gvec[0:1, :] = jnp.sum(grad * scaled, axis=0, keepdims=True)
    gvec[1:2, :] = jnp.sum(grad, axis=0, keepdims=True)


def second_back(chunks, middle, cotangent, gain, places):
    count, width = cotangent.shape
    return pl.pallas_call(
        second_back_kernel,
        out_shape=[
            jax.ShapeDtypeStruct((count, width), F32),
            jax.ShapeDtypeStruct((count, width), BF),
            jax.ShapeDtypeStruct((8, width), F32),
        ],
        compiler_params=params(32),
        cost_estimate=cost(4 * count * count * width, 16 * count * width),
        name="second_back",
    )(*chunks, middle, cotangent, gain, places)


def output_kernel(*refs):
    chunks = refs[:CHUNKS]
    middle, gate, places, out = refs[CHUNKS:]
    out[...] = (middle[...] + gate[...] * take_chunks(chunks, places[...])).astype(BF)


def output_call(chunks, middle, gate, places):
    return pl.pallas_call(
        output_kernel,
        out_shape=jax.ShapeDtypeStruct(middle.shape, BF),
        compiler_params=params(32),
        cost_estimate=cost(4 * middle.shape[0] * middle.size, 8 * middle.size),
        name="output",
    )(*chunks, middle, gate, places)


def attend_back_kernel(
    heads, last_group, info, own, oth, rows, weight, outw, att, qkv, recip, probs, *refs
):
    if last_group:
        before, gweight, gout, kept, sent, gbranch, gatt, gqkv = refs
    else:
        gweight, gout, gnormed, gbranch, gatt, gqkv = refs
    length = PACKED_LENGTH
    step = pl.program_id(0)
    width = heads * HEAD_DIM
    blk = length // 4
    half = length // 2

    @pl.when(step == 0)
    def start():
        parity = info[0]
        for ref, place in ((own, parity), (oth, 1 - parity)):
            gbranch[pl.ds(pl.multiple_of(place * half, half), half), :] = ref[...]
        gatt[...] = dot(outw[...], gbranch[...], 1, 1).astype(BF)
        gout[...] = dot(att[...], gbranch[...], 1, 0).astype(BF)
        gqkv[...] = jnp.zeros_like(gqkv)

    for index in range(4):

        @pl.when(step == index)
        def block(index=index):
            upto = (index + 1) * blk
            cols = slice(index * blk, upto)
            for head in range(heads):
                at = head * HEAD_DIM
                here = slice(at, at + HEAD_DIM)
                kat = slice(width + at, width + at + HEAD_DIM)
                vat = slice(2 * width + at, 2 * width + at + HEAD_DIM)
                query, keys, values = qkv[here, cols], qkv[kat, 0:upto], qkv[vat, 0:upto]
                grad = (gatt[here, cols].astype(F32) * recip[head : head + 1, cols]).astype(BF)
                inner = jnp.sum(
                    grad.astype(F32) * att[here, cols].astype(F32), axis=0, keepdims=True
                )
                low = probs[head, 0:upto, :]
                gprobs = dot(values, grad, 0, 0)
                gscores = (low.astype(F32) * (gprobs - inner)).astype(BF)
                gqkv[vat, 0:upto] += dot(grad, low, 1, 1)
                gqkv[kat, 0:upto] += dot(query, gscores, 1, 1)
                gqkv[here, cols] = dot(keys, gscores, 1, 0) * HEAD_DIM**-0.5

    @pl.when(step == 3)
    def finish():
        grads = gqkv[...].astype(BF)
        gweight[...] = dot(grads, rows[...], 1, 0).astype(BF)
        if last_group:
            parity = info[0]
            for ref, place in ((sent, 1 - parity), (kept, parity)):
                at = pl.ds(pl.multiple_of(place * half, half), half)
                gqkv_low = gqkv[:, at].astype(BF)
                total = dot(gqkv_low, weight[...], 0, 0) + before[at, :]
                ref[...] = total.astype(ref.dtype)
        else:
            gnormed[...] = dot(grads, weight[...], 0, 0)


def attend_back(info, own, oth, rows, weight, outw, att, qkv, recip, probs, before=None):
    length, model = rows.shape
    width = att.shape[0]
    heads = width // HEAD_DIM
    blk = length // 4
    whole = lambda shape: pl.BlockSpec(shape, lambda i: (0,) * len(shape))
    operands = [own, oth, rows, weight, outw, att, qkv, recip, probs]
    in_specs = [smem()] + [whole(o.shape) for o in operands[:-1]]
    in_specs.append(pl.BlockSpec((heads, length, blk), lambda i: (0, 0, i)))
    shapes = [((3 * width, model), BF), ((width, model), BF)]
    if before is None:
        shapes.append(((length, model), F32))
    else:
        operands.append(before)
        in_specs.append(whole(before.shape))
        shapes += [((length // 2, model), F32), ((length // 2, model), BF)]
    return pl.pallas_call(
        functools.partial(attend_back_kernel, heads, before is not None),
        out_shape=[jax.ShapeDtypeStruct(s, d) for s, d in shapes],
        grid=(4,),
        in_specs=in_specs,
        out_specs=[whole(s) for s, d in shapes],
        scratch_shapes=[
            pltpu.VMEM((length, model), BF),
            pltpu.VMEM((width, length), BF),
            pltpu.VMEM((3 * width, length), F32),
        ],
        compiler_params=params(48, dimension_semantics=("arbitrary",)),
        cost_estimate=cost(
            16 * length * model * width + 16 * heads * length * length * HEAD_DIM,
            2 * heads * length * length + 10 * length * model,
        ),
        name="attend_back",
    )(info, *operands)


def first_back_kernel(tokens, gmid, kept, received, gain, ginput, gvec):
    grad = kept[...] + received[...].astype(F32)
    scaled, inverse = norm_parts(tokens[...].astype(F32))
    ginput[...] = gmid[...] + norm_back(grad, scaled, inverse, gain[...])
    gvec[...] = jnp.zeros_like(gvec)
    gvec[0:1, :] = jnp.sum(grad * scaled, axis=0, keepdims=True)
    gvec[1:2, :] = jnp.sum(grad, axis=0, keepdims=True)


def first_back(tokens, gmid, kept, received, gain):
    count, width = tokens.shape
    return pl.pallas_call(
        first_back_kernel,
        out_shape=[
            jax.ShapeDtypeStruct((count, width), F32),
            jax.ShapeDtypeStruct((8, width), F32),
        ],
        compiler_params=params(32),
        cost_estimate=cost(20 * count * width, 16 * count * width),
        name="first_back",
    )(tokens, gmid, kept, received, gain)


def swap(values, axis, bit):
    pairs = [(i, i ^ bit) for i in range(lax.axis_size(axis))]
    return lax.ppermute(values, axis, pairs)


def expert_groups(count):
    return [[2 * e + k for e in range(count)] for k in range(2)]


def exchange(blocks, count, here):
    if count == len(blocks):
        return [blocks[0]] + [swap(b, "dp", 2 * s) for s, b in enumerate(blocks) if s > 0]
    whole = jnp.concatenate(blocks, axis=0)
    order = here ^ jnp.arange(count, dtype=jnp.int32)
    shaped = whole.reshape(count, -1, whole.shape[1])[order]
    moved = lax.all_to_all(
        shaped, "dp", 0, 0, tiled=True, axis_index_groups=expert_groups(count)
    )
    moved = moved[order].reshape(whole.shape)
    size = whole.shape[0] // len(blocks)
    return [moved[i * size : (i + 1) * size] for i in range(len(blocks))]


def sum_all(values, axes):
    for axis in axes:
        bit = 1
        while bit < lax.axis_size(axis):
            values = values + swap(values, axis, bit)
            bit *= 2
    return values


def sum_dp(values, count, here, k):
    rows, columns = values.shape
    half = rows // 2
    low = values.astype(BF)
    gone = lax.dynamic_slice_in_dim(low, (1 - k) * half, half, 0)
    kept = lax.dynamic_slice_in_dim(values, k * half, half, 0)
    kept = kept + swap(gone, "dp", 1).astype(F32)
    piece = half // count
    if count <= 4:
        low = kept.astype(BF)
        total = lax.dynamic_slice_in_dim(kept, here * piece, piece, 0)
        for s in range(1, count):
            block = lax.dynamic_slice_in_dim(low, (here ^ s) * piece, piece, 0)
            total = total + swap(block, "dp", 2 * s).astype(F32)
        total = total.astype(BF)
        full = jnp.zeros((half, columns), BF)
        full = lax.dynamic_update_slice_in_dim(full, total, here * piece, 0)
        for s in range(1, count):
            full = lax.dynamic_update_slice_in_dim(
                full, swap(total, "dp", 2 * s), (here ^ s) * piece, 0
            )
    else:
        groups = expert_groups(count)
        blocks = kept.astype(BF).reshape(count, piece, columns)
        blocks = lax.all_to_all(blocks, "dp", 0, 0, tiled=True, axis_index_groups=groups)
        total = jnp.sum(blocks.astype(F32), axis=0).astype(BF)
        full = lax.all_gather(total, "dp", axis=0, tiled=True, axis_index_groups=groups)
    other = swap(full, "dp", 1)
    first, second = jnp.where(k == 0, full, other), jnp.where(k == 0, other, full)
    return jnp.concatenate([first, second], axis=0).astype(F32)


def local(
    tokens,
    first_gain,
    first_bias,
    qkv_weight,
    out_weight,
    second_gain,
    expert_norm_bias,
    up_weight,
    down_weight,
    gate_value,
    expert_ids,
    slot_index,
    segment_ids,
    cotangent,
):
    count, model = tokens.shape
    width = qkv_weight.shape[2]
    tp = lax.axis_index("tp")
    dp = lax.axis_index("dp")
    parity = tp % 2
    row_half = tp // 2 % 2
    k = dp % 2
    here = dp // 2
    experts = lax.axis_size("dp") // 2
    capacity = 2 * count // experts
    info = jnp.stack([parity, here]).astype(jnp.int32)
    vector = lambda v: v.reshape(1, model)

    other_tokens = swap(tokens, "tp", 1)
    other_segments = swap(segment_ids, "tp", 1)
    weight_a = jnp.transpose(qkv_weight, (1, 2, 0)).reshape(3 * width, model)
    weight_b = swap(weight_a, "tp", 2)
    out_b = swap(out_weight, "tp", 2)
    tile = up_weight.shape[2] // 2
    sub = tile // 2
    up_sub = up_weight.reshape(model, 2, 2, sub)
    down_sub = down_weight.reshape(2, 2, sub, model)

    def pick(which):
        up = lax.dynamic_index_in_dim(up_sub, which, 2, keepdims=False).reshape(model, tile)
        down = lax.dynamic_index_in_dim(down_sub, which, 1, keepdims=False).reshape(tile, model)
        return up, down

    up0, down0 = pick(parity)
    up1, down1 = pick(1 - parity)
    up2, down2 = swap(up0, "dp", 1), swap(down0, "dp", 1)
    up3, down3 = swap(up2, "tp", 1), swap(down2, "tp", 1)
    ups, downs = (up0, up1, up2, up3), (down0, down1, down2, down3)

    places = ((expert_ids ^ here) * capacity + slot_index).reshape(1, count)
    gate = gate_value.reshape(count, 1)
    sent_grads = grad_dispatch(cotangent, gate, places)
    grads = exchange(sent_grads, experts, here)

    segments = jnp.where(
        parity == 0,
        jnp.concatenate([segment_ids, other_segments]),
        jnp.concatenate([other_segments, segment_ids]),
    )
    segr, segc = segments.reshape(1, -1), segments.reshape(-1, 1)
    gain, bias = vector(first_gain), vector(first_bias)
    rows, att_a, probs_a, qkv_a, recip_a = attend(
        True, info, tokens, other_tokens, gain, bias, weight_a, segr, segc
    )
    att_b, probs_b, qkv_b, recip_b = attend(
        False, info, rows, other_segments.reshape(1, -1), gain, bias, weight_b, segr, segc
    )
    kept, sent = project(info, att_a, att_b, out_weight, out_b)
    received = swap(sent, "tp", 1)
    middle, *sent_rows = middle_call(
        tokens, kept, received, vector(second_gain), vector(expert_norm_bias), places
    )

    inputs = exchange(sent_rows, experts, here)
    hiddens, gpres, backs = [], [], []
    for index in range(CHUNKS):
        hidden, gpre, back = expert(inputs[index], grads[index], ups, downs)
        hiddens.append(hidden)
        gpres.append(gpre)
        backs.append(back)
    returned = exchange(backs, experts, here)
    *results, gup, gdown = expert_weights(inputs, grads, hiddens, gpres, downs)
    gmid, gbranch, gvec_two = second_back(
        returned, middle, cotangent, vector(second_gain), places
    )
    outs = exchange(results, experts, here)
    output = output_call(outs, middle, gate, places)

    def over_cores(values):
        return [
            (values[i].astype(F32) + swap(values[i + 1], "tp", 1).astype(F32)).astype(BF)
            for i in (0, 2)
        ]

    gup_mine, gup_other = over_cores(gup)
    gdown_mine, gdown_other = over_cores(gdown)
    gup_mine = gup_mine.astype(F32) + swap(gup_other, "dp", 1).astype(F32)
    gdown_mine = gdown_mine.astype(F32) + swap(gdown_other, "dp", 1).astype(F32)

    def over_rows(values, axis):
        away = lax.dynamic_slice_in_dim(values, (1 - row_half) * sub, sub, axis)
        stays = lax.dynamic_slice_in_dim(values, row_half * sub, sub, axis)
        return stays + swap(away.astype(BF), "tp", 2).astype(F32)

    grad_up = over_rows(gup_mine, 1)[None]
    grad_down = over_rows(gdown_mine, 0)[None]

    other_branch = swap(gbranch, "tp", 1)
    gweight_b, gout_b, before = attend_back(
        info, gbranch, other_branch, rows, weight_b, out_b, att_b, qkv_b, recip_b, probs_b
    )
    gweight_a, gout_a, gkept, gsent = attend_back(
        info, gbranch, other_branch, rows, weight_a, out_weight, att_a, qkv_a, recip_a, probs_a,
        before,
    )
    greceived = swap(gsent, "tp", 1)
    grad_input, gvec_one = first_back(tokens, gmid, gkept, greceived, gain)
    theirs_weight = swap(gweight_b, "tp", 2)
    theirs_out = swap(gout_b, "tp", 2)
    gweight = gweight_a.astype(F32) + theirs_weight.astype(F32)
    gout = gout_a.astype(F32) + theirs_out.astype(F32)
    summed = sum_dp(jnp.concatenate([gweight, gout], axis=0), experts, here, k)
    grad_qkv = jnp.transpose(summed[: 3 * width].reshape(3, width, model), (2, 0, 1))
    grad_out = summed[3 * width :]
    vec_two = sum_all(gvec_two, ("tp", "dp"))
    vec_one = sum_all(gvec_one, ("tp", "dp"))
    return (
        output,
        grad_input,
        vec_one[0],
        vec_one[1],
        grad_qkv,
        grad_out,
        vec_two[0],
        vec_two[1],
        grad_up,
        grad_down,
    )


def solution(mesh):
    placed = (
        P(("dp", "tp"), None),
        P(),
        P(),
        P(None, None, "tp"),
        P("tp", None),
        P(),
        P(),
        P("dp", None, None),
        P("dp", None, None),
        P(("dp", "tp")),
        P(("dp", "tp")),
        P(("dp", "tp")),
        P(("dp", "tp")),
        P(("dp", "tp"), None),
    )
    return jax.shard_map(
        local,
        mesh=mesh,
        in_specs=placed,
        out_specs=(
            P(("dp", "tp"), None),
            P(("dp", "tp"), None),
            P(),
            P(),
            P(None, None, "tp"),
            P("tp", None),
            P(),
            P(),
            P("dp", None, "tp"),
            P("dp", "tp", None),
        ),
        check_vma=False,
    )
```

time: 850 us -> 428 us (0.50)
  waiting for transfers between devices: 372 us -> 114 us
  matrix products: 211 us -> 0 us
  Pallas kernels: 0 us -> 128 us
  starting transfers between devices: 19.4 us -> 103 us
  local copies, waits for them, and re-layouts: 102 us -> 50 us
  blocking collectives: 49.5 us -> 0 us
  other arithmetic: 56.2 us -> 22.4 us
  loops' own time: 13.6 us -> 0 us
  between operations: 15.1 us -> 1.69 us
    all_to_all x4 -> x0, waiting for transfers between devices: 225 us -> none  [the longest x1 66.9 us: local(): lax.all_to_all(dispatch(normed_two), 'dp', split_axis=0, concat_axis=0, t...]
    dot_general x40 -> x0, matrix products: 211 us -> none  [the longest x1 35.6 us: expert_forward(): jnp.einsum('secf,efd->secd', hidden, down_weight, preferred_element_type=...]
    pallas_call x0 -> x15, Pallas kernels: none -> 128 us  [the longest x4 40.1 us: expert(): pl.pallas_call(functools.partial(expert_kernel, tiles), out_shape=[jax.Sh...]
    ppermute x0 -> x51, waiting for transfers between devices: none -> 114 us  [swap(): return lax.ppermute(values, axis, pairs)]
    ppermute x0 -> x51, starting transfers between devices: none -> 103 us  [swap(): return lax.ppermute(values, axis, pairs)]
    psum x1 -> x0, waiting for transfers between devices: 65.9 us -> none  [local(): lax.psum((grad_qkv_weight, grad_out_weight), 'dp')]
    reduce_scatter x3 -> x0, waiting for transfers between devices: 55.8 us -> none  [the longest x1 38.1 us: local(): lax.psum_scatter(jnp.dot(attended, out_weight, preferred_element_type=jnp...]
    psum x1 -> x0, blocking collectives: 43.2 us -> none  [local(): lax.psum((grad_first_gain, grad_first_bias, grad_second_gain, grad_second...]
  transfers between devices with their start and end apart: 11 -> 51, of which waited for: 8 -> 19; matrix products, arithmetic and copies ran while one was open for 28% -> 13% of each run, Pallas kernels for 0% -> 30%
where the time goes in v1:
time: 428 us; the launch traced here: 419 us
  Pallas kernels  128 us (30%)
  waiting for transfers between devices  114 us (27%)
  starting transfers between devices  103 us (24%)
  local copies, waits for them, and re-layouts  50 us (12%)
  other arithmetic  22.4 us (5%)
    ppermute x51, waiting for transfers between devices, swap(): return lax.ppermute(values, axis, pairs)  114 us
    ppermute x51, starting transfers between devices, swap(): return lax.ppermute(values, axis, pairs)  103 us
    pallas_call x4, Pallas kernels, expert(): pl.pallas_call(functools.partial(expert_kernel, tiles), out_shape=[jax.Sh...  40.1 us
    pallas_call x2, Pallas kernels, attend_back(): pl.pallas_call(functools.partial(attend_back_kernel, heads, before is not...  27 us
    pallas_call x1, Pallas kernels, expert_weights(): pl.pallas_call(functools.partial(expert_weights_kernel, tiles), out_shape...  25.2 us
    pallas_call x2, Pallas kernels, attend(): pl.pallas_call(functools.partial(attend_kernel, first, heads), out_shape=...  21.4 us
    dynamic_slice x1, local copies, waits for them, and re-layouts, pick(): lax.dynamic_index_in_dim(up_sub, which, 2, keepdims=False)  16.4 us
    unnamed x114, local copies, waits for them, and re-layouts  15.4 us
  transfers between devices with their start and end apart: 51, of which 19 were waited for; matrix products, arithmetic and copies ran while one was open for 13% of the time, Pallas kernels for 30%

profile of v1, /device:TPU:0, one launch (start us, length us, event | category | flops | bytes accessed | tf_op | source)
XLA Modules:
  0.0 419.2 jit_solution(9763324362513765296)
XLA Ops:
  1.2 2.9 collective-permute-start.2
  4.2 4.9 %reshape.197 = bf16[768,2,2,384]{3,2,1,0:T(2,128)(2,1)S(1)} reshape(bf16[1,768,1536]{2,1,0:T(8,128)(2,1)} %param.21) | data formatting | bytes 4718592 | tf_op jit(solution)/shard_map/reshape | solution.py:626
  9.1 16.4 %dynamic-slice_reduce_fusion = (bf16[768,2,384]{2,1,0:T(2,128)(2,1)}, bf16[768,2,384]{2,1,0:T(2,128)(2,1)S(1)}) fusion(bf16[768,2,2,384]{3,2,1,0:T(2,128)(2,1)S(1)} %reshape.197, s32[]{:T(128)S(6)} %select_n.107, s32[]{:T(128)S(6)} %select_n.106), kind=kLoop, calls=%fused_computation.15 | loop fusion | bytes 4718600 | tf_op jit(solution)/shard_map/jit(dynamic_index_in_dim)/dynamic_slice | solution.py:630
  25.8 1.6 collective-permute-start.11
  27.4 1.6 constant_dynamic-slice_fusion.3
  35.5 11.2 %attend.2 = (bf16[1024,768]{1,0:T(8,128)(2,1)S(1)}, bf16[192,1024]{1,0:T(8,128)(2,1)S(1)}, bf16[3,1024,1024]{2,1,0:T(8,128)(2,1)S(1)}, bf16[576,1024]{1,0:T(8,128)(2,1)S(1)}, f32[8,1024]{1,0:T(8,128)S(1)}) custom-call(s32[2]{0:T(128)S(1)} %pad_add_fusion.2.info, bf16[512,768]{1,0:T(8,128)(2,1)S(1)} %copy-done, bf16[512,768]{1,0:T(8,128)(2,1)} %collective-permute-done.oth, ...), custom_call_target="tpu_custom_call" | custom-call | flops 2516582400 | bytes 11010048 | tf_op jit(solution)/shard_map/attend/pallas_call | solution.py:170
  46.7 2.6 copy-done.30
  51.0 10.2 %attend.3 = (bf16[192,1024]{1,0:T(8,128)(2,1)S(1)}, bf16[3,1024,1024]{2,1,0:T(8,128)(2,1)S(1)}, bf16[576,1024]{1,0:T(8,128)(2,1)S(1)}, f32[8,1024]{1,0:T(8,128)S(1)}) custom-call(s32[2]{0:T(128)S(1)} %pad_add_fusion.2.info, bf16[1024,768]{1,0:T(8,128)(2,1)S(1)} %get-tuple-element.61.own.rows, s32[1,512]{1,0:T(1,128)S(1)} %bitcast.70, ...), custom_call_target="tpu_custom_call" | custom-call | flops 2516582400 | bytes 11010048 | tf_op jit(solution)/shard_map/attend/pallas_call | solution.py:170
  61.2 2.7 copy-done.31
  64.6 3.3 project.1
  69.6 9.4 %collective-permute-done.13.refs_6_ = bf16[768,768]{1,0:T(8,128)(2,1)} collective-permute-done((bf16[768,768]{1,0:T(8,128)(2,1)}, bf16[768,768]{1,0:T(8,128)(2,1)}, u32[]{:S(2)}, u32[]{:S(2)}) %collective-permute-start.13) | collective-permute-done | bytes 1179680 | tf_op jit(solution)/shard_map/ppermute | solution.py:528
  80.3 3.7 collective-permute-start.10
  84.0 2.8 middle.1
  87.9 6.3 %collective-permute-done.10.grads.refs_7_ = bf16[256,768]{1,0:T(8,128)(2,1)S(1)} collective-permute-done((bf16[256,768]{1,0:T(8,128)(2,1)S(1)}, bf16[256,768]{1,0:T(8,128)(2,1)S(1)}, u32[]{:S(2)}, u32[]{:S(2)}) %collective-permute-start.10) | collective-permute-done | bytes 393248 | tf_op jit(solution)/shard_map/ppermute | solution.py:528
  94.2 26.0 %collective-permute-start.6 = (bf16[256,768]{1,0:T(8,128)(2,1)S(1)}, bf16[256,768]{1,0:T(8,128)(2,1)S(1)}, u32[]{:S(2)}, u32[]{:S(2)}) collective-permute-start(bf16[256,768]{1,0:T(8,128)(2,1)S(1)} %get-tuple-element.67), channel_id=1, source_target_pairs={{0,16},{4,20},{8,24},{12,28},{16,0},{20,4},{24,8},{28,12},{1,17},{... | collective-permute-start | bytes 1179656 | tf_op jit(solution)/shard_map/ppermute | solution.py:528
  120.4 15.6 %collective-permute-start.8 = (bf16[256,768]{1,0:T(8,128)(2,1)S(1)}, bf16[256,768]{1,0:T(8,128)(2,1)S(1)}, u32[]{:S(2)}, u32[]{:S(2)}) collective-permute-start(bf16[256,768]{1,0:T(8,128)(2,1)S(1)} %get-tuple-element.70), channel_id=1, source_target_pairs={{0,8},{4,12},{8,0},{12,4},{16,24},{20,28},{24,16},{28,20},{1,9},{5... | collective-permute-start | bytes 1179656 | tf_op jit(solution)/shard_map/ppermute | solution.py:528
  136.0 10.1 %expert.7 = (bf16[256,3072]{1,0:T(8,128)(2,1)}, bf16[256,3072]{1,0:T(8,128)(2,1)}, bf16[256,768]{1,0:T(8,128)(2,1)S(1)}) custom-call(bf16[256,768]{1,0:T(8,128)(2,1)S(1)} %collective-permute-done.7.inputs.refs_3_, bf16[256,768]{1,0:T(8,128)(2,1)S(1)} %collective-permute-done.10.grads.refs_7_, bf16[768,768]{1,0:T(8,128)(2,1)S(1)} %bitcast.56, ...), custom_call_target="tpu_custom_call" | custom-call | flops 3623878656 | bytes 12582912 | tf_op jit(solution)/shard_map/expert/pallas_call | solution.py:275
  146.1 2.5 collective-permute-start.20
  148.6 3.7 collective-permute-done.6.inputs.refs_2_
  152.3 9.9 %expert.6 = (bf16[256,3072]{1,0:T(8,128)(2,1)}, bf16[256,3072]{1,0:T(8,128)(2,1)}, bf16[256,768]{1,0:T(8,128)(2,1)S(1)}) custom-call(bf16[256,768]{1,0:T(8,128)(2,1)S(1)} %collective-permute-done.6.inputs.refs_2_, bf16[256,768]{1,0:T(8,128)(2,1)S(1)} %collective-permute-done.9.grads.refs_6_, bf16[768,768]{1,0:T(8,128)(2,1)S(1)} %bitcast.57, ...), custom_call_target="tpu_custom_call" | custom-call | flops 3623878656 | bytes 12582912 | tf_op jit(solution)/shard_map/expert/pallas_call | solution.py:275
  162.2 6.6 %collective-permute-done.8.grads.refs_5_ = bf16[256,768]{1,0:T(8,128)(2,1)S(1)} collective-permute-done((bf16[256,768]{1,0:T(8,128)(2,1)S(1)}, bf16[256,768]{1,0:T(8,128)(2,1)S(1)}, u32[]{:S(2)}, u32[]{:S(2)}) %collective-permute-start.8) | collective-permute-done | bytes 393248 | tf_op jit(solution)/shard_map/ppermute | solution.py:528
  168.8 8.7 %collective-permute-done.5.inputs.refs_1_ = bf16[256,768]{1,0:T(8,128)(2,1)S(1)} collective-permute-done((bf16[256,768]{1,0:T(8,128)(2,1)S(1)}, bf16[256,768]{1,0:T(8,128)(2,1)S(1)}, u32[]{:S(2)}, u32[]{:S(2)}) %collective-permute-start.5) | collective-permute-done | bytes 393248 | tf_op jit(solution)/shard_map/ppermute | solution.py:528
  177.5 10.1 %expert.5 = (bf16[256,3072]{1,0:T(8,128)(2,1)}, bf16[256,3072]{1,0:T(8,128)(2,1)}, bf16[256,768]{1,0:T(8,128)(2,1)S(1)}) custom-call(bf16[256,768]{1,0:T(8,128)(2,1)S(1)} %collective-permute-done.5.inputs.refs_1_, bf16[256,768]{1,0:T(8,128)(2,1)S(1)} %collective-permute-done.8.grads.refs_5_, bf16[768,768]{1,0:T(8,128)(2,1)S(1)} %bitcast.58, ...), custom_call_target="tpu_custom_call" | custom-call | flops 3623878656 | bytes 12582912 | tf_op jit(solution)/shard_map/expert/pallas_call | solution.py:275
  187.6 9.9 %expert.4 = (bf16[256,3072]{1,0:T(8,128)(2,1)}, bf16[256,3072]{1,0:T(8,128)(2,1)}, bf16[256,768]{1,0:T(8,128)(2,1)S(1)}) custom-call(bf16[256,768]{1,0:T(8,128)(2,1)S(1)} %get-tuple-element.65.inputs.refs_0_, bf16[256,768]{1,0:T(8,128)(2,1)S(1)} %get-tuple-element.69.grads.refs_4_, bf16[768,768]{1,0:T(8,128)(2,1)S(1)} %bitcast.59, ...), custom_call_target="tpu_custom_call" | custom-call | flops 3623878656 | bytes 12582912 | tf_op jit(solution)/shard_map/expert/pallas_call | solution.py:275
  197.6 4.2 pad_maximum_fusion.refs_16_
  201.8 1.8 second_back.1
  204.7 25.2 %expert_weights.1 = (bf16[256,768]{1,0:T(8,128)(2,1)S(1)}, bf16[256,768]{1,0:T(8,128)(2,1)S(1)}, bf16[256,768]{1,0:T(8,128)(2,1)S(1)}, bf16[256,768]{1,0:T(8,128...) custom-call(bf16[256,768]{1,0:T(8,128)(2,1)S(1)} %get-tuple-element.65.inputs.refs_0_, ...), custom_call_target="tpu_custom_call" | custom-call | flops 14495514624 | bytes 18874368 | tf_op jit(solution)/shard_map/expert_weights/pallas_call | solution.py:338
  230.0 3.7 slice_bitcast_fusion.1
  234.4 13.2 %attend_back.2 = (bf16[576,768]{1,0:T(8,128)(2,1)}, bf16[192,768]{1,0:T(8,128)(2,1)S(1)}, f32[1024,768]{1,0:T(8,128)}) custom-call(s32[2]{0:T(128)S(1)} %pad_add_fusion.2.info, bf16[512,768]{1,0:T(8,128)(2,1)S(1)} %get-tuple-element.91.own, bf16[512,768]{1,0:T(8,128)(2,1)S(1)} %collective-permute-done.21.oth, bf16[1024,768]{1,0:T(8,128)(2,1)} %copy-done.32, ...), custom_call_target="tpu_custom_call" | custom-call | flops 5637144576 | bytes 14155776 | tf_op jit(solution)/shard_map/attend_back/pallas_call | solution.py:483
  247.6 13.8 %attend_back.3 = (bf16[576,768]{1,0:T(8,128)(2,1)S(1)}, bf16[192,768]{1,0:T(8,128)(2,1)S(1)}, f32[512,768]{1,0:T(8,128)}, bf16[512,768]{1,0:T(8,128)(2,1)}) custom-call(s32[2]{0:T(128)S(1)} %pad_add_fusion.2.info, bf16[512,768]{1,0:T(8,128)(2,1)S(1)} %get-tuple-element.91.own, bf16[512,768]{1,0:T(8,128)(2,1)S(1)} %collective-permute-done.21.oth, ...), custom_call_target="tpu_custom_call" | custom-call | flops 5637144576 | bytes 14155776 | tf_op jit(solution)/shard_map/attend_back/pallas_call | solution.py:483
  262.0 1.5 collective-permute-done.38
  264.6 1.5 collective-permute-start.28
  266.1 1.6 slice_bitcast_fusion.3
  268.5 2.0 collective-permute-start.15
  274.4 3.6 first_back.1
  278.1 3.1 fusion
  281.1 11.9 %collective-permute-done.29 = bf16[192,768]{1,0:T(8,128)(2,1)S(1)} collective-permute-done((bf16[192,768]{1,0:T(8,128)(2,1)}, bf16[192,768]{1,0:T(8,128)(2,1)S(1)}, u32[]{:S(2)}, u32[]{:S(2)}) %collective-permute-start.29) | collective-permute-done | bytes 294944 | tf_op jit(solution)/shard_map/ppermute | solution.py:528
  293.0 3.0 collective-permute-start.16
  297.6 1.6 collective-permute-start.49
  300.6 22.2 %collective-permute-done.16.refs_2_ = bf16[256,768]{1,0:T(8,128)(2,1)S(1)} collective-permute-done((bf16[256,768]{1,0:T(8,128)(2,1)S(1)}, bf16[256,768]{1,0:T(8,128)(2,1)S(1)}, u32[]{:S(2)}, u32[]{:S(2)}) %collective-permute-start.16) | collective-permute-done | bytes 393248 | tf_op jit(solution)/shard_map/ppermute | solution.py:528
  322.8 1.5 collective-permute-start.40
  326.7 1.5 collective-permute-start.30
  328.2 6.2 %collective-permute-start.41 = (f32[8,768]{1,0:T(8,128)S(1)}, f32[8,768]{1,0:T(8,128)S(1)}, u32[]{:S(2)}, u32[]{:S(2)}) collective-permute-start(f32[8,768]{1,0:T(8,128)S(1)} %add.152), channel_id=1, source_target_pairs={{0,8},{4,12},{8,0},{12,4},{16,24},{20,28},{24,16},{28,20},{1,9},{5... | collective-permute-start | bytes 73736 | tf_op jit(solution)/shard_map/ppermute | solution.py:528
  334.4 1.8 collective-permute-done.41
  336.2 1.5 collective-permute-start.25
  337.8 4.7 %collective-permute-done.25 = f32[8,768]{1,0:T(8,128)S(1)} collective-permute-done((f32[8,768]{1,0:T(8,128)S(1)}, f32[8,768]{1,0:T(8,128)S(1)}, u32[]{:S(2)}, u32[]{:S(2)}) %collective-permute-start.25) | collective-permute-done | bytes 24608 | tf_op jit(solution)/shard_map/ppermute | solution.py:528
  342.5 5.1 %collective-permute-start.42 = (f32[8,768]{1,0:T(8,128)S(1)}, f32[8,768]{1,0:T(8,128)S(1)}, u32[]{:S(2)}, u32[]{:S(2)}) collective-permute-start(f32[8,768]{1,0:T(8,128)S(1)} %add.153), channel_id=1, source_target_pairs={{0,16},{4,20},{8,24},{12,28},{16,0},{20,4},{24,8},{28,12},{1,17},{... | collective-permute-start | bytes 73736 | tf_op jit(solution)/shard_map/ppermute | solution.py:528
  347.5 1.8 collective-permute-done.42
  349.3 2.7 collective-permute-start.26
  354.0 2.0 output.1
  356.7 2.0 fusion.2
  358.7 2.2 collective-permute-done.27
  360.9 1.5 collective-permute-start.45
  363.5 2.5 collective-permute-start.32
  366.0 1.8 collective-permute-start.33
  367.9 2.4 convert_add_fusion.4
  371.7 5.5 %collective-permute-done.32 = bf16[96,768]{1,0:T(8,128)(2,1)S(1)} collective-permute-done((bf16[96,768]{1,0:T(8,128)(2,1)S(1)}, bf16[96,768]{1,0:T(8,128)(2,1)S(1)}, u32[]{:S(2)}, u32[]{:S(2)}) %collective-permute-start.32) | collective-permute-done | bytes 147488 | tf_op jit(solution)/shard_map/ppermute | solution.py:528
  377.4 2.5 collective-permute-start.34
  379.9 8.4 %collective-permute-done.45 = bf16[768,768]{1,0:T(8,128)(2,1)S(1)} collective-permute-done((bf16[768,768]{1,0:T(8,128)(2,1)S(1)}, bf16[768,768]{1,0:T(8,128)(2,1)S(1)}, u32[]{:S(2)}, u32[]{:S(2)}) %collective-permute-start.45) | collective-permute-done | bytes 1179680 | tf_op jit(solution)/shard_map/ppermute | solution.py:528
  388.3 1.8 convert_add_fusion.5
  392.2 1.9 collective-permute-start.36
  394.2 8.3 %collective-permute-done.35 = bf16[96,768]{1,0:T(8,128)(2,1)S(1)} collective-permute-done((bf16[96,768]{1,0:T(8,128)(2,1)S(1)}, bf16[96,768]{1,0:T(8,128)(2,1)S(1)}, u32[]{:S(2)}, u32[]{:S(2)}) %collective-permute-start.35) | collective-permute-done | bytes 147488 | tf_op jit(solution)/shard_map/ppermute | solution.py:528
  402.5 1.6 collective-permute-start.37
  407.0 9.5 %collective-permute-done.37 = bf16[384,768]{1,0:T(8,128)(2,1)S(1)} collective-permute-done((bf16[384,768]{1,0:T(8,128)(2,1)S(1)}, bf16[384,768]{1,0:T(8,128)(2,1)S(1)}, u32[]{:S(2)}, u32[]{:S(2)}) %collective-permute-start.37) | collective-permute-done | bytes 589856 | tf_op jit(solution)/shard_map/ppermute | solution.py:528
  (220 shorter events, 40.6 us)
Async XLA Ops:
  0.6 31.1 %collective-permute-start.1 = (s32[512]{0:T(512)}, s32[512]{0:T(512)S(1)}, u32[]{:S(2)}, u32[]{:S(2)}) collective-permute-start(s32[512]{0:T(512)} %param.26), channel_id=1, source_target_pairs={{0,1},{1,0},{2,3},{3,2},{4,5},{5,4},{6,7},{7,6},{8,9},{9,8},{10,11... | collective-permute-start | bytes 6152 | tf_op jit(solution)/shard_map/ppermute | solution.py:528
  1.2 34.3 %collective-permute-start = (bf16[512,768]{1,0:T(8,128)(2,1)}, bf16[512,768]{1,0:T(8,128)(2,1)}, u32[]{:S(2)}, u32[]{:S(2)}) collective-permute-start(bf16[512,768]{1,0:T(8,128)(2,1)} %tokens.3), channel_id=1, source_target_pairs={{0,1},{1,0},{2,3},{3,2},{4,5},{5,4},{6,7},{7,6},{8,9},{9,8},{10,11... | collective-permute-start | bytes 2359304 | tf_op jit(solution)/shard_map/ppermute | solution.py:528
  1.2 49.7 %collective-permute-start.2 = (bf16[576,768]{1,0:T(8,128)(2,1)}, bf16[576,768]{1,0:T(8,128)(2,1)}, u32[]{:S(2)}, u32[]{:S(2)}) collective-permute-start(bf16[576,768]{1,0:T(8,128)(2,1)} %bitcast.71), channel_id=1, source_target_pairs={{0,2},{1,3},{2,0},{3,1},{4,6},{5,7},{6,4},{7,5},{8,10},{9,11},{10,... | collective-permute-start | bytes 2654216 | tf_op jit(solution)/shard_map/ppermute | solution.py:528
  25.8 43.2 %collective-permute-start.11 = (bf16[768,768]{1,0:T(8,128)(2,1)S(1)}, bf16[768,768]{1,0:T(8,128)(2,1)}, u32[]{:S(2)}, u32[]{:S(2)}) collective-permute-start(bf16[768,768]{1,0:T(8,128)(2,1)S(1)} %bitcast.55), channel_id=1, source_target_pairs={{0,4},{4,0},{8,12},{12,8},{16,20},{20,16},{24,28},{28,24},{1,5},{5... | collective-permute-start | bytes 3538952 | tf_op jit(solution)/shard_map/ppermute | solution.py:528
  28.9 50.0 %collective-permute-start.13 = (bf16[768,768]{1,0:T(8,128)(2,1)}, bf16[768,768]{1,0:T(8,128)(2,1)}, u32[]{:S(2)}, u32[]{:S(2)}) collective-permute-start(bf16[768,768]{1,0:T(8,128)(2,1)} %bitcast.12.refs_4_), channel_id=1, source_target_pairs={{0,4},{4,0},{8,12},{12,8},{16,20},{20,16},{24,28},{28,24},{1,5},{5... | collective-permute-start | bytes 3538952 | tf_op jit(solution)/shard_map/ppermute | solution.py:528
  31.7 32.8 %collective-permute-start.3 = (bf16[192,768]{1,0:T(8,128)(2,1)}, bf16[192,768]{1,0:T(8,128)(2,1)}, u32[]{:S(2)}, u32[]{:S(2)}) collective-permute-start(bf16[192,768]{1,0:T(8,128)(2,1)} %outw.1), channel_id=1, source_target_pairs={{0,2},{1,3},{2,0},{3,1},{4,6},{5,7},{6,4},{7,5},{8,10},{9,11},{10,... | collective-permute-start | bytes 884744 | tf_op jit(solution)/shard_map/ppermute | solution.py:528
  64.5 14.6 %copy-start.53 = (s32[512]{0:T(512)S(1)}, s32[512]{0:T(512)}, u32[]{:S(2)}) copy-start(s32[512]{0:T(512)} %param.24) | copy-start | bytes 6148
  64.6 14.6 %copy-start.8 = (bf16[512,768]{1,0:T(8,128)(2,1)S(1)}, bf16[512,768]{1,0:T(8,128)(2,1)}, u32[]{:S(2)}) copy-start(bf16[512,768]{1,0:T(8,128)(2,1)} %refs_5_.1) | copy-start | bytes 2359300
  69.0 14.9 %collective-permute-start.4 = (bf16[512,768]{1,0:T(8,128)(2,1)}, bf16[512,768]{1,0:T(8,128)(2,1)}, u32[]{:S(2)}, u32[]{:S(2)}) collective-permute-start(bf16[512,768]{1,0:T(8,128)(2,1)} %get-tuple-element.64), channel_id=1, source_target_pairs={{0,1},{1,0},{2,3},{3,2},{4,5},{5,4},{6,7},{7,6},{8,9},{9,8},{10,11... | collective-permute-start | bytes 2359304 | tf_op jit(solution)/shard_map/ppermute | solution.py:528
  69.0 66.9 %collective-permute-start.12 = (bf16[768,768]{1,0:T(8,128)(2,1)}, bf16[768,768]{1,0:T(8,128)(2,1)}, u32[]{:S(2)}, u32[]{:S(2)}) collective-permute-start(bf16[768,768]{1,0:T(8,128)(2,1)} %collective-permute-done.11.refs_2_), channel_id=1, source_target_pairs={{0,1},{1,0},{2,3},{3,2},{4,5},{5,4},{6,7},{7,6},{8,9},{9,8},{10,11... | collective-permute-start | bytes 3538952 | tf_op jit(solution)/shard_map/ppermute | solution.py:528
  78.9 57.1 %collective-permute-start.14 = (bf16[768,768]{1,0:T(8,128)(2,1)}, bf16[768,768]{1,0:T(8,128)(2,1)}, u32[]{:S(2)}, u32[]{:S(2)}) collective-permute-start(bf16[768,768]{1,0:T(8,128)(2,1)} %collective-permute-done.13.refs_6_), channel_id=1, source_target_pairs={{0,1},{1,0},{2,3},{3,2},{4,5},{5,4},{6,7},{7,6},{8,9},{9,8},{10,11... | collective-permute-start | bytes 3538952 | tf_op jit(solution)/shard_map/ppermute | solution.py:528
  80.3 13.9 %collective-permute-start.10 = (bf16[256,768]{1,0:T(8,128)(2,1)S(1)}, bf16[256,768]{1,0:T(8,128)(2,1)S(1)}, u32[]{:S(2)}, u32[]{:S(2)}) collective-permute-start(bf16[256,768]{1,0:T(8,128)(2,1)S(1)} %get-tuple-element.72), channel_id=1, source_target_pairs={{0,24},{4,28},{8,16},{12,20},{16,8},{20,12},{24,0},{28,4},{1,25},{... | collective-permute-start | bytes 1179656 | tf_op jit(solution)/shard_map/ppermute | solution.py:528
  84.0 36.1 %copy-start.45 = (bf16[768,2,384]{2,1,0:T(2,128)(2,1)S(1)}, bf16[768,2,384]{2,1,0:T(2,128)(2,1)}, u32[]{:S(2)}) copy-start(bf16[768,2,384]{2,1,0:T(2,128)(2,1)} %get-tuple-element.110) | copy-start | bytes 3538948
  86.8 33.6 %collective-permute-start.7 = (bf16[256,768]{1,0:T(8,128)(2,1)S(1)}, bf16[256,768]{1,0:T(8,128)(2,1)S(1)}, u32[]{:S(2)}, u32[]{:S(2)}) collective-permute-start(bf16[256,768]{1,0:T(8,128)(2,1)S(1)} %get-tuple-element.68), channel_id=1, source_target_pairs={{0,24},{4,28},{8,16},{12,20},{16,8},{20,12},{24,0},{28,4},{1,25},{... | collective-permute-start | bytes 1179656 | tf_op jit(solution)/shard_map/ppermute | solution.py:528
  87.1 61.5 %collective-permute-start.9 = (bf16[256,768]{1,0:T(8,128)(2,1)S(1)}, bf16[256,768]{1,0:T(8,128)(2,1)S(1)}, u32[]{:S(2)}, u32[]{:S(2)}) collective-permute-start(bf16[256,768]{1,0:T(8,128)(2,1)S(1)} %get-tuple-element.71), channel_id=1, source_target_pairs={{0,16},{4,20},{8,24},{12,28},{16,0},{20,4},{24,8},{28,12},{1,17},{... | collective-permute-start | bytes 1179656 | tf_op jit(solution)/shard_map/ppermute | solution.py:528
  94.2 58.2 %collective-permute-start.6 = (bf16[256,768]{1,0:T(8,128)(2,1)S(1)}, bf16[256,768]{1,0:T(8,128)(2,1)S(1)}, u32[]{:S(2)}, u32[]{:S(2)}) collective-permute-start(bf16[256,768]{1,0:T(8,128)(2,1)S(1)} %get-tuple-element.67), channel_id=1, source_target_pairs={{0,16},{4,20},{8,24},{12,28},{16,0},{20,4},{24,8},{28,12},{1,17},{... | collective-permute-start | bytes 1179656 | tf_op jit(solution)/shard_map/ppermute | solution.py:528
  120.4 48.4 %collective-permute-start.8 = (bf16[256,768]{1,0:T(8,128)(2,1)S(1)}, bf16[256,768]{1,0:T(8,128)(2,1)S(1)}, u32[]{:S(2)}, u32[]{:S(2)}) collective-permute-start(bf16[256,768]{1,0:T(8,128)(2,1)S(1)} %get-tuple-element.70), channel_id=1, source_target_pairs={{0,8},{4,12},{8,0},{12,4},{16,24},{20,28},{24,16},{28,20},{1,9},{5... | collective-permute-start | bytes 1179656 | tf_op jit(solution)/shard_map/ppermute | solution.py:528
  136.0 41.5 %collective-permute-start.5 = (bf16[256,768]{1,0:T(8,128)(2,1)S(1)}, bf16[256,768]{1,0:T(8,128)(2,1)S(1)}, u32[]{:S(2)}, u32[]{:S(2)}) collective-permute-start(bf16[256,768]{1,0:T(8,128)(2,1)S(1)} %get-tuple-element.66), channel_id=1, source_target_pairs={{0,8},{4,12},{8,0},{12,4},{16,24},{20,28},{24,16},{28,20},{1,9},{5... | collective-permute-start | bytes 1179656 | tf_op jit(solution)/shard_map/ppermute | solution.py:528
  146.1 55.6 %collective-permute-start.20 = (bf16[256,768]{1,0:T(8,128)(2,1)S(1)}, bf16[256,768]{1,0:T(8,128)(2,1)S(1)}, u32[]{:S(2)}, u32[]{:S(2)}) collective-permute-start(bf16[256,768]{1,0:T(8,128)(2,1)S(1)} %get-tuple-element.89), channel_id=1, source_target_pairs={{0,24},{4,28},{8,16},{12,20},{16,8},{20,12},{24,0},{28,4},{1,25},{... | collective-permute-start | bytes 1179656 | tf_op jit(solution)/shard_map/ppermute | solution.py:528
  162.2 39.6 %collective-permute-start.19 = (bf16[256,768]{1,0:T(8,128)(2,1)S(1)}, bf16[256,768]{1,0:T(8,128)(2,1)S(1)}, u32[]{:S(2)}, u32[]{:S(2)}) collective-permute-start(bf16[256,768]{1,0:T(8,128)(2,1)S(1)} %get-tuple-element.88), channel_id=1, source_target_pairs={{0,16},{4,20},{8,24},{12,28},{16,0},{20,4},{24,8},{28,12},{1,17},{... | collective-permute-start | bytes 1179656 | tf_op jit(solution)/shard_map/ppermute | solution.py:528
  187.6 14.2 %collective-permute-start.18 = (bf16[256,768]{1,0:T(8,128)(2,1)S(1)}, bf16[256,768]{1,0:T(8,128)(2,1)S(1)}, u32[]{:S(2)}, u32[]{:S(2)}) collective-permute-start(bf16[256,768]{1,0:T(8,128)(2,1)S(1)} %get-tuple-element.87), channel_id=1, source_target_pairs={{0,8},{4,12},{8,0},{12,4},{16,24},{20,28},{24,16},{28,20},{1,9},{5... | collective-permute-start | bytes 1179656 | tf_op jit(solution)/shard_map/ppermute | solution.py:528
  204.7 29.6 %collective-permute-start.21 = (bf16[512,768]{1,0:T(8,128)(2,1)S(1)}, bf16[512,768]{1,0:T(8,128)(2,1)S(1)}, u32[]{:S(2)}, u32[]{:S(2)}) collective-permute-start(bf16[512,768]{1,0:T(8,128)(2,1)S(1)} %get-tuple-element.91.own), channel_id=1, source_target_pairs={{0,1},{1,0},{2,3},{3,2},{4,5},{5,4},{6,7},{7,6},{8,9},{9,8},{10,11... | collective-permute-start | bytes 2359304 | tf_op jit(solution)/shard_map/ppermute | solution.py:528
  233.8 44.2 %collective-permute-start.48 = (bf16[768,768]{1,0:T(8,128)(2,1)}, bf16[768,768]{1,0:T(8,128)(2,1)}, u32[]{:S(2)}, u32[]{:S(2)}) collective-permute-start(bf16[768,768]{1,0:T(8,128)(2,1)} %get-tuple-element.121), channel_id=1, source_target_pairs={{0,1},{1,0},{2,3},{3,2},{4,5},{5,4},{6,7},{7,6},{8,9},{9,8},{10,11... | collective-permute-start | bytes 3538952 | tf_op jit(solution)/shard_map/ppermute | solution.py:528
  247.6 18.6 %slice-start = ((s8[4718592]{0:T(1024)(128)(4,1)}), s8[4194304]{0:T(1024)(128)(4,1)S(1)}, s32[]{:S(2)}) async-start(s8[4718592]{0:T(1024)(128)(4,1)} %bitcast.79), calls=%async_computation | async-start | bytes 8388608
  247.6 18.6 %slice-start.1 = ((s8[4718592]{0:T(1024)(128)(4,1)}), s8[524288]{0:T(1024)(128)(4,1)S(1)}, s32[]{:S(2)}) async-start(s8[4718592]{0:T(1024)(128)(4,1)} %bitcast.79), calls=%async_computation.1 | async-start | bytes 1048576
  261.4 9.8 %collective-permute-start.22 = (bf16[512,768]{1,0:T(8,128)(2,1)}, bf16[512,768]{1,0:T(8,128)(2,1)}, u32[]{:S(2)}, u32[]{:S(2)}) collective-permute-start(bf16[512,768]{1,0:T(8,128)(2,1)} %get-tuple-element.100), channel_id=1, source_target_pairs={{0,1},{1,0},{2,3},{3,2},{4,5},{5,4},{6,7},{7,6},{8,9},{9,8},{10,11... | collective-permute-start | bytes 2359304 | tf_op jit(solution)/shard_map/ppermute | solution.py:528
  261.5 2.0 collective-permute-start.38
  264.1 4.4 %collective-permute-start.39 = (f32[8,768]{1,0:T(8,128)}, f32[8,768]{1,0:T(8,128)}, u32[]{:S(2)}, u32[]{:S(2)}) collective-permute-start(f32[8,768]{1,0:T(8,128)} %add.150), channel_id=1, source_target_pairs={{0,2},{1,3},{2,0},{3,1},{4,6},{5,7},{6,4},{7,5},{8,10},{9,11},{10,... | collective-permute-start | bytes 73736 | tf_op jit(solution)/shard_map/ppermute | solution.py:528
  264.6 33.0 %collective-permute-start.28 = (bf16[576,768]{1,0:T(8,128)(2,1)}, bf16[576,768]{1,0:T(8,128)(2,1)}, u32[]{:S(2)}, u32[]{:S(2)}) collective-permute-start(bf16[576,768]{1,0:T(8,128)(2,1)} %get-tuple-element.104), channel_id=1, source_target_pairs={{0,2},{1,3},{2,0},{3,1},{4,6},{5,7},{6,4},{7,5},{8,10},{9,11},{10,... | collective-permute-start | bytes 2654216 | tf_op jit(solution)/shard_map/ppermute | solution.py:528
  267.7 88.4 %collective-permute-start.44 = (bf16[768,768]{1,0:T(8,128)(2,1)}, bf16[768,768]{1,0:T(8,128)(2,1)}, u32[]{:S(2)}, u32[]{:S(2)}) collective-permute-start(bf16[768,768]{1,0:T(8,128)(2,1)} %get-tuple-element.123), channel_id=1, source_target_pairs={{0,1},{1,0},{2,3},{3,2},{4,5},{5,4},{6,7},{7,6},{8,9},{9,8},{10,11... | collective-permute-start | bytes 3538952 | tf_op jit(solution)/shard_map/ppermute | solution.py:528
  268.5 29.0 %collective-permute-start.15 = (bf16[256,768]{1,0:T(8,128)(2,1)}, bf16[256,768]{1,0:T(8,128)(2,1)S(1)}, u32[]{:S(2)}, u32[]{:S(2)}) collective-permute-start(bf16[256,768]{1,0:T(8,128)(2,1)} %copy-done.24), channel_id=1, source_target_pairs={{0,8},{4,12},{8,0},{12,4},{16,24},{20,28},{24,16},{28,20},{1,9},{5... | collective-permute-start | bytes 1179656 | tf_op jit(solution)/shard_map/ppermute | solution.py:528
  271.2 21.8 %collective-permute-start.29 = (bf16[192,768]{1,0:T(8,128)(2,1)}, bf16[192,768]{1,0:T(8,128)(2,1)S(1)}, u32[]{:S(2)}, u32[]{:S(2)}) collective-permute-start(bf16[192,768]{1,0:T(8,128)(2,1)} %copy-done.25), channel_id=1, source_target_pairs={{0,2},{1,3},{2,0},{3,1},{4,6},{5,7},{6,4},{7,5},{8,10},{9,11},{10,... | collective-permute-start | bytes 884744 | tf_op jit(solution)/shard_map/ppermute | solution.py:528
  278.0 15.1 %copy-start.23 = (bf16[256,768]{1,0:T(8,128)(2,1)S(1)}, bf16[256,768]{1,0:T(8,128)(2,1)}, u32[]{:S(2)}) copy-start(bf16[256,768]{1,0:T(8,128)(2,1)} %copy-done.22) | copy-start | bytes 1179652
  278.0 18.1 %copy-start.21 = (bf16[256,768]{1,0:T(8,128)(2,1)S(1)}, bf16[256,768]{1,0:T(8,128)(2,1)}, u32[]{:S(2)}) copy-start(bf16[256,768]{1,0:T(8,128)(2,1)} %copy-done.20) | copy-start | bytes 1179652
  278.0 18.1 %collective-permute-start.23 = (f32[8,768]{1,0:T(8,128)S(1)}, f32[8,768]{1,0:T(8,128)S(1)}, u32[]{:S(2)}, u32[]{:S(2)}) collective-permute-start(f32[8,768]{1,0:T(8,128)S(1)} %get-tuple-element.102), channel_id=1, source_target_pairs={{0,1},{1,0},{2,3},{3,2},{4,5},{5,4},{6,7},{7,6},{8,9},{9,8},{10,11... | collective-permute-start | bytes 73736 | tf_op jit(solution)/shard_map/ppermute | solution.py:528
  293.0 29.8 %collective-permute-start.16 = (bf16[256,768]{1,0:T(8,128)(2,1)S(1)}, bf16[256,768]{1,0:T(8,128)(2,1)S(1)}, u32[]{:S(2)}, u32[]{:S(2)}) collective-permute-start(bf16[256,768]{1,0:T(8,128)(2,1)S(1)} %copy-done.23), channel_id=1, source_target_pairs={{0,16},{4,20},{8,24},{12,28},{16,0},{20,4},{24,8},{28,12},{1,17},{... | collective-permute-start | bytes 1179656 | tf_op jit(solution)/shard_map/ppermute | solution.py:528
  296.0 28.3 %collective-permute-start.17 = (bf16[256,768]{1,0:T(8,128)(2,1)S(1)}, bf16[256,768]{1,0:T(8,128)(2,1)S(1)}, u32[]{:S(2)}, u32[]{:S(2)}) collective-permute-start(bf16[256,768]{1,0:T(8,128)(2,1)S(1)} %copy-done.21), channel_id=1, source_target_pairs={{0,24},{4,28},{8,16},{12,20},{16,8},{20,12},{24,0},{28,4},{1,25},{... | collective-permute-start | bytes 1179656 | tf_op jit(solution)/shard_map/ppermute | solution.py:528
  297.5 27.8 %copy-start.42 = (f32[192,768]{1,0:T(8,128)}, f32[192,768]{1,0:T(8,128)S(1)}, u32[]{:S(2)}) copy-start(f32[192,768]{1,0:T(8,128)S(1)} %convert_add_fusion.7) | copy-start | bytes 1769476
  297.5 66.0 %collective-permute-start.47 = (bf16[768,768]{1,0:T(8,128)(2,1)}, bf16[768,768]{1,0:T(8,128)(2,1)}, u32[]{:S(2)}, u32[]{:S(2)}) collective-permute-start(bf16[768,768]{1,0:T(8,128)(2,1)} %get-tuple-element.120), channel_id=1, source_target_pairs={{0,1},{1,0},{2,3},{3,2},{4,5},{5,4},{6,7},{7,6},{8,9},{9,8},{10,11... | collective-permute-start | bytes 3538952 | tf_op jit(solution)/shard_map/ppermute | solution.py:528
  297.6 68.4 %collective-permute-start.49 = (bf16[768,768]{1,0:T(8,128)(2,1)}, bf16[768,768]{1,0:T(8,128)(2,1)}, u32[]{:S(2)}, u32[]{:S(2)}) collective-permute-start(bf16[768,768]{1,0:T(8,128)(2,1)} %fusion), channel_id=1, source_target_pairs={{0,4},{4,0},{8,12},{12,8},{16,20},{20,16},{24,28},{28,24},{1,5},{5... | collective-permute-start | bytes 3538952 | tf_op jit(solution)/shard_map/ppermute | solution.py:528
  300.6 37.2 %copy-start.40 = (f32[576,768]{1,0:T(8,128)}, f32[576,768]{1,0:T(8,128)S(1)}, u32[]{:S(2)}) copy-start(f32[576,768]{1,0:T(8,128)S(1)} %convert_add_fusion.6) | copy-start | bytes 5308420
  300.6 51.4 %copy-start.7 = (f32[512,1]{1,0:T(8,128)S(1)}, f32[512,1]{1,0:T(8,128)}, u32[]{:S(2)}) copy-start(f32[512,1]{1,0:T(8,128)} %copy-done.6) | copy-start | bytes 6148
  300.6 51.4 %copy-start.11 = (bf16[256,768]{1,0:T(8,128)(2,1)S(1)}, bf16[256,768]{1,0:T(8,128)(2,1)}, u32[]{:S(2)}) copy-start(bf16[256,768]{1,0:T(8,128)(2,1)} %copy-done.10) | copy-start | bytes 1179652
  322.8 15.0 %copy-start.14 = (bf16[256,768]{1,0:T(8,128)(2,1)}, bf16[256,768]{1,0:T(8,128)(2,1)S(1)}, u32[]{:S(2)}) copy-start(bf16[256,768]{1,0:T(8,128)(2,1)S(1)} %collective-permute-done.16.refs_2_) | copy-start | bytes 1179652
  322.8 29.2 %copy-start.13 = (bf16[256,768]{1,0:T(8,128)(2,1)S(1)}, bf16[256,768]{1,0:T(8,128)(2,1)}, u32[]{:S(2)}) copy-start(bf16[256,768]{1,0:T(8,128)(2,1)} %copy-done.12) | copy-start | bytes 1179652
  322.8 3.9 collective-permute-start.40
  324.3 3.9 collective-permute-start.24
  326.7 36.3 %collective-permute-start.30 = (bf16[384,768]{1,0:T(8,128)(2,1)}, bf16[384,768]{1,0:T(8,128)(2,1)S(1)}, u32[]{:S(2)}, u32[]{:S(2)}) collective-permute-start(bf16[384,768]{1,0:T(8,128)(2,1)} %fusion.5), channel_id=1, source_target_pairs={{0,4},{4,0},{8,12},{12,8},{16,20},{20,16},{24,28},{28,24},{1,5},{5... | collective-permute-start | bytes 1769480 | tf_op jit(solution)/shard_map/ppermute | solution.py:528
  328.2 8.0 %collective-permute-start.41 = (f32[8,768]{1,0:T(8,128)S(1)}, f32[8,768]{1,0:T(8,128)S(1)}, u32[]{:S(2)}, u32[]{:S(2)}) collective-permute-start(f32[8,768]{1,0:T(8,128)S(1)} %add.152), channel_id=1, source_target_pairs={{0,8},{4,12},{8,0},{12,4},{16,24},{20,28},{24,16},{28,20},{1,9},{5... | collective-permute-start | bytes 73736 | tf_op jit(solution)/shard_map/ppermute | solution.py:528
  336.2 6.2 %collective-permute-start.25 = (f32[8,768]{1,0:T(8,128)S(1)}, f32[8,768]{1,0:T(8,128)S(1)}, u32[]{:S(2)}, u32[]{:S(2)}) collective-permute-start(f32[8,768]{1,0:T(8,128)S(1)} %add.133), channel_id=1, source_target_pairs={{0,4},{4,0},{8,12},{12,8},{16,20},{20,16},{24,28},{28,24},{1,5},{5... | collective-permute-start | bytes 73736 | tf_op jit(solution)/shard_map/ppermute | solution.py:528
  342.5 6.9 %collective-permute-start.42 = (f32[8,768]{1,0:T(8,128)S(1)}, f32[8,768]{1,0:T(8,128)S(1)}, u32[]{:S(2)}, u32[]{:S(2)}) collective-permute-start(f32[8,768]{1,0:T(8,128)S(1)} %add.153), channel_id=1, source_target_pairs={{0,16},{4,20},{8,24},{12,28},{16,0},{20,4},{24,8},{28,12},{1,17},{... | collective-permute-start | bytes 73736 | tf_op jit(solution)/shard_map/ppermute | solution.py:528
  349.3 6.6 %collective-permute-start.26 = (f32[8,768]{1,0:T(8,128)S(1)}, f32[8,768]{1,0:T(8,128)S(1)}, u32[]{:S(2)}, u32[]{:S(2)}) collective-permute-start(f32[8,768]{1,0:T(8,128)S(1)} %add.134), channel_id=1, source_target_pairs={{0,8},{4,12},{8,0},{12,4},{16,24},{20,28},{24,16},{28,20},{1,9},{5... | collective-permute-start | bytes 73736 | tf_op jit(solution)/shard_map/ppermute | solution.py:528
  355.9 23.9 %collective-permute-start.43 = (bf16[768,768]{1,0:T(8,128)(2,1)S(1)}, bf16[768,768]{1,0:T(8,128)(2,1)S(1)}, u32[]{:S(2)}, u32[]{:S(2)}) collective-permute-start(bf16[768,768]{1,0:T(8,128)(2,1)S(1)} %copy-done.47), channel_id=1, source_target_pairs={{0,1},{1,0},{2,3},{3,2},{4,5},{5,4},{6,7},{7,6},{8,9},{9,8},{10,11... | collective-permute-start | bytes 3538952 | tf_op jit(solution)/shard_map/ppermute | solution.py:528
  356.1 4.8 %collective-permute-start.27 = (f32[8,768]{1,0:T(8,128)S(1)}, f32[8,768]{1,0:T(8,128)S(1)}, u32[]{:S(2)}, u32[]{:S(2)}) collective-permute-start(f32[8,768]{1,0:T(8,128)S(1)} %add.135), channel_id=1, source_target_pairs={{0,16},{4,20},{8,24},{12,28},{16,0},{20,4},{24,8},{28,12},{1,17},{... | collective-permute-start | bytes 73736 | tf_op jit(solution)/shard_map/ppermute | solution.py:528
  360.9 27.4 %collective-permute-start.45 = (bf16[768,768]{1,0:T(8,128)(2,1)S(1)}, bf16[768,768]{1,0:T(8,128)(2,1)S(1)}, u32[]{:S(2)}, u32[]{:S(2)}) collective-permute-start(bf16[768,768]{1,0:T(8,128)(2,1)S(1)} %fusion.2), channel_id=1, source_target_pairs={{0,4},{4,0},{8,12},{12,8},{16,20},{20,16},{24,28},{28,24},{1,5},{5... | collective-permute-start | bytes 3538952 | tf_op jit(solution)/shard_map/ppermute | solution.py:528
  363.4 7.1 %collective-permute-start.31 = (bf16[96,768]{1,0:T(8,128)(2,1)S(1)}, bf16[96,768]{1,0:T(8,128)(2,1)S(1)}, u32[]{:S(2)}, u32[]{:S(2)}) collective-permute-start(bf16[96,768]{1,0:T(8,128)(2,1)S(1)} %get-tuple-element.128), channel_id=1, source_target_pairs={{0,8},{4,12},{8,0},{12,4},{16,24},{20,28},{24,16},{28,20},{1,9},{5... | collective-permute-start | bytes 442376 | tf_op jit(solution)/shard_map/ppermute | solution.py:528
  363.5 13.8 %collective-permute-start.32 = (bf16[96,768]{1,0:T(8,128)(2,1)S(1)}, bf16[96,768]{1,0:T(8,128)(2,1)S(1)}, u32[]{:S(2)}, u32[]{:S(2)}) collective-permute-start(bf16[96,768]{1,0:T(8,128)(2,1)S(1)} %get-tuple-element.130), channel_id=1, source_target_pairs={{0,16},{4,20},{8,24},{12,28},{16,0},{20,4},{24,8},{28,12},{1,17},{... | collective-permute-start | bytes 442376 | tf_op jit(solution)/shard_map/ppermute | solution.py:528
  366.0 11.2 %collective-permute-start.33 = (bf16[96,768]{1,0:T(8,128)(2,1)S(1)}, bf16[96,768]{1,0:T(8,128)(2,1)S(1)}, u32[]{:S(2)}, u32[]{:S(2)}) collective-permute-start(bf16[96,768]{1,0:T(8,128)(2,1)S(1)} %get-tuple-element.129), channel_id=1, source_target_pairs={{0,24},{4,28},{8,16},{12,20},{16,8},{20,12},{24,0},{28,4},{1,25},{... | collective-permute-start | bytes 442376 | tf_op jit(solution)/shard_map/ppermute | solution.py:528
  370.6 34.1 %collective-permute-start.50 = (bf16[384,768]{1,0:T(8,128)(2,1)S(1)}, bf16[384,768]{1,0:T(8,128)(2,1)S(1)}, u32[]{:S(2)}, u32[]{:S(2)}) collective-permute-start(bf16[384,768]{1,0:T(8,128)(2,1)S(1)} %dynamic-slice_convert_fusion), channel_id=1, source_target_pairs={{0,2},{1,3},{2,0},{3,1},{4,6},{5,7},{6,4},{7,5},{8,10},{9,11},{10,... | collective-permute-start | bytes 1769480 | tf_op jit(solution)/shard_map/ppermute | solution.py:528
  377.4 16.7 %collective-permute-start.34 = (bf16[96,768]{1,0:T(8,128)(2,1)S(1)}, bf16[96,768]{1,0:T(8,128)(2,1)S(1)}, u32[]{:S(2)}, u32[]{:S(2)}) collective-permute-start(bf16[96,768]{1,0:T(8,128)(2,1)S(1)} %get-tuple-element.117), channel_id=1, source_target_pairs={{0,8},{4,12},{8,0},{12,4},{16,24},{20,28},{24,16},{28,20},{1,9},{5... | collective-permute-start | bytes 442376 | tf_op jit(solution)/shard_map/ppermute | solution.py:528
  390.1 12.4 %collective-permute-start.35 = (bf16[96,768]{1,0:T(8,128)(2,1)S(1)}, bf16[96,768]{1,0:T(8,128)(2,1)S(1)}, u32[]{:S(2)}, u32[]{:S(2)}) collective-permute-start(bf16[96,768]{1,0:T(8,128)(2,1)S(1)} %get-tuple-element.117), channel_id=1, source_target_pairs={{0,16},{4,20},{8,24},{12,28},{16,0},{20,4},{24,8},{28,12},{1,17},{... | collective-permute-start | bytes 442376 | tf_op jit(solution)/shard_map/ppermute | solution.py:528
  391.0 14.8 %collective-permute-start.46 = (bf16[768,384]{1,0:T(8,128)(2,1)S(1)}, bf16[768,384]{1,0:T(8,128)(2,1)S(1)}, u32[]{:S(2)}, u32[]{:S(2)}) collective-permute-start(bf16[768,384]{1,0:T(8,128)(2,1)S(1)} %dynamic-slice_convert_fusion.1), channel_id=1, source_target_pairs={{0,2},{1,3},{2,0},{3,1},{4,6},{5,7},{6,4},{7,5},{8,10},{9,11},{10,... | collective-permute-start | bytes 1769480 | tf_op jit(solution)/shard_map/ppermute | solution.py:528
  392.2 10.3 %collective-permute-start.36 = (bf16[96,768]{1,0:T(8,128)(2,1)S(1)}, bf16[96,768]{1,0:T(8,128)(2,1)S(1)}, u32[]{:S(2)}, u32[]{:S(2)}) collective-permute-start(bf16[96,768]{1,0:T(8,128)(2,1)S(1)} %get-tuple-element.117), channel_id=1, source_target_pairs={{0,24},{4,28},{8,16},{12,20},{16,8},{20,12},{24,0},{28,4},{1,25},{... | collective-permute-start | bytes 442376 | tf_op jit(solution)/shard_map/ppermute | solution.py:528
  402.5 13.9 %collective-permute-start.37 = (bf16[384,768]{1,0:T(8,128)(2,1)S(1)}, bf16[384,768]{1,0:T(8,128)(2,1)S(1)}, u32[]{:S(2)}, u32[]{:S(2)}) collective-permute-start(bf16[384,768]{1,0:T(8,128)(2,1)S(1)} %constant_dynamic-update-slice_fusion), channel_id=1, source_target_pairs={{0,4},{4,0},{8,12},{12,8},{16,20},{20,16},{24,28},{28,24},{1,5},{5... | collective-permute-start | bytes 1769480 | tf_op jit(solution)/shard_map/ppermute | solution.py:528
  (43 other events, 264.1 us)
